TPU v7x, 256 devices: a whole 4x4x8 slice. The times are simulated.
256 devices in a mesh: dp: 32 (over x, z), expert: 8 (over y, core).
Axes of the slice: x: 4, y: 4, z: 8, core: 2. Of those that a mesh axis runs over, the one named last changes fastest.
Arguments:
- tokens: bfloat16 [4096, 4096], P('dp', 'expert'), may hold values from -6 to 6
- cotangent: bfloat16 [4096, 4096], P('dp', 'expert'), may hold values from -6 to 6
- expert_ids: int32 [4096, 8], P('dp'), may hold values from 0 to 63, all different within a row; in each aligned block of 128 rows (0 to 127, 128 to 255, ...) at most 24 rows name the same one
- gate_values: float32 [4096, 8], P('dp'), may hold values from 0.05 to 0.5
- swap_plan: int32 [32], replicated, may hold values from 0 to 1, as said below
- gate_weight: bfloat16 [64, 4096, 768], P('dp', 'expert'), may hold values from -0.09375 to 0.09375
- up_weight: bfloat16 [64, 4096, 768], P('dp', 'expert'), may hold values from -0.09375 to 0.09375
- down_weight: bfloat16 [64, 768, 4096], P('dp', None, 'expert'), may hold values from -0.21875 to 0.21875
Outputs:
- token_grad: bfloat16 [4096, 4096], P('dp', 'expert')
- gate_grad: bfloat16 [64, 4096, 768], P('dp', 'expert')
- up_grad: bfloat16 [64, 4096, 768], P('dp', 'expert')
- down_grad: bfloat16 [64, 768, 4096], P('dp', None, 'expert')
Inputs may be any that keep to these rules, and one draw needn't show every extreme that they name: `expert_ids`: in each aligned block of 128 rows (the tokens of one dp index) no expert is named by more than 24 rows; the 8 experts of a row are distinct. swap_plan[p] equals swap_plan[p + 16] for p < 16.
All inputs are finite; a program needn't handle non-finite values.
Results may differ from a plain program's by a relative error of at most 0.0058.
Values may be sent and summed in bfloat16 or wider, within the bound.
A program may use at most 128 MiB of HBM per device.

v0:
```python
import jax
import jax.numpy as jnp
from jax import lax
from jax.sharding import PartitionSpec as P


def from_partner(block, axis, stride):
    count = lax.axis_size(axis)
    route = []
    for low in range(count):
        high = low | 1 << stride
        if high != low and high < count:
            route += [(low, high), (high, low)]
    return lax.ppermute(block, axis, route)


def shards(
    tokens, cotangent, expert_ids, gate_values, swap_plan, gate_weight, up_weight, down_weight
):
    dp_size = lax.axis_size("dp")
    my_host = lax.axis_index("dp")
    pair_bit = dp_size.bit_length() - 2
    half_way = dp_size // 2
    per_host, width_part, hidden_width = gate_weight.shape
    tok_rows, top_count = expert_ids.shape
    most_rows = 6 * tok_rows // dp_size
    rows_all = dp_size * most_rows
    slot_count = rows_all * per_host
    last_slot = per_host - 1
    flagged = swap_plan[my_host] == 1
    home_host = expert_ids // per_host
    sub_slot = expert_ids % per_host
    moved_in = from_partner(
        (gate_weight[last_slot], up_weight[last_slot], down_weight[last_slot]), "dp", pair_bit
    )
    gate_w = gate_weight.at[last_slot].set(jnp.where(flagged, moved_in[0], gate_weight[last_slot]))
    up_w = up_weight.at[last_slot].set(jnp.where(flagged, moved_in[1], up_weight[last_slot]))
    down_w = down_weight.at[last_slot].set(jnp.where(flagged, moved_in[2], down_weight[last_slot]))
    shifted = (sub_slot == last_slot) & (swap_plan[home_host] == 1)
    target_host = jnp.where(shifted, (home_host + half_way) % dp_size, home_host)
    experts_all = per_host * dp_size
    route_ids = expert_ids.reshape(-1)
    onehot = (route_ids[:, None] == jnp.arange(experts_all, dtype=jnp.int32)[None, :]).astype(
        jnp.int32
    )
    ranks = jnp.sum(jnp.cumsum(onehot, axis=0) * onehot, axis=1) - 1
    flat_slot = (target_host.reshape(-1) * most_rows + ranks) * per_host + sub_slot.reshape(-1)
    owner = (
        jnp.full((slot_count,), -1, jnp.int32)
        .at[flat_slot]
        .set(jnp.arange(tok_rows * top_count, dtype=jnp.int32))
    )
    filled = (owner >= 0)[:, None]
    source = jnp.maximum(owner, 0)
    routed = (gate_values[:, :, None] * cotangent[:, None, :].astype(jnp.float32)).astype(
        jnp.bfloat16
    )
    routed = routed.reshape(tok_rows * top_count, width_part)
    token_send = jnp.where(filled, tokens[source // top_count], jnp.zeros((), jnp.bfloat16))
    routed_send = jnp.where(filled, routed[source], jnp.zeros((), jnp.bfloat16))
    token_send = token_send.reshape(dp_size, most_rows, per_host, width_part)
    routed_send = routed_send.reshape(dp_size, most_rows, per_host, width_part)
    x_rows, g_rows = (
        lax.all_to_all(token_send, "dp", split_axis=0, concat_axis=0, tiled=True),
        lax.all_to_all(routed_send, "dp", split_axis=0, concat_axis=0, tiled=True),
    )
    x_rows = x_rows.reshape(rows_all, per_host, width_part)
    g_rows = g_rows.reshape(rows_all, per_host, width_part)
    x_part = x_rows
    gate_pre = jnp.einsum("rsd,sdf->rsf", x_part, gate_w, preferred_element_type=jnp.float32)
    up_pre = jnp.einsum("rsd,sdf->rsf", x_part, up_w, preferred_element_type=jnp.float32)
    g_part = g_rows
    sums = lax.psum_scatter(
        jnp.concatenate(
            [
                jnp.concatenate([gate_pre, up_pre], axis=2),
                jnp.einsum("rsd,sfd->rsf", g_part, down_w, preferred_element_type=jnp.float32),
            ],
            axis=2,
        ),
        "expert",
        scatter_dimension=0,
        tiled=True,
    )
    gate_pre = sums[:, :, :hidden_width]
    up_pre = sums[:, :, hidden_width : 2 * hidden_width]
    back = sums[:, :, 2 * hidden_width :]
    sig = jax.nn.sigmoid(gate_pre)
    silu = gate_pre * sig
    hidden_act = silu * up_pre
    gate_delta = back * up_pre * sig * (1.0 + gate_pre * (1.0 - sig))
    up_delta = back * silu
    acts = jnp.concatenate([hidden_act, gate_delta, up_delta], axis=2).astype(jnp.bfloat16)
    piece = lax.all_gather(acts, "expert", axis=0, tiled=True)
    x_part = x_rows
    g_part = g_rows
    hid_part = piece[:, :, :hidden_width]
    gate_part = piece[:, :, hidden_width : 2 * hidden_width]
    up_part = piece[:, :, 2 * hidden_width :]
    gate_acc = jnp.einsum("rsd,rsf->sdf", x_part, gate_part, preferred_element_type=jnp.float32)
    up_acc = jnp.einsum("rsd,rsf->sdf", x_part, up_part, preferred_element_type=jnp.float32)
    down_acc = jnp.einsum("rsf,rsd->sfd", hid_part, g_part, preferred_element_type=jnp.float32)
    token_part = jnp.einsum("rsf,sdf->rsd", gate_part, gate_w, preferred_element_type=jnp.float32)
    token_part = token_part + jnp.einsum(
        "rsf,sdf->rsd", up_part, up_w, preferred_element_type=jnp.float32
    )
    rows_acc = token_part
    gate_acc, up_acc, down_acc, rows_acc = (gate_acc, up_acc, down_acc, rows_acc)
    returned = lax.all_to_all(
        rows_acc.reshape(dp_size, most_rows, per_host, width_part),
        "dp",
        split_axis=0,
        concat_axis=0,
        tiled=True,
    )
    returned = returned.reshape(slot_count, width_part)
    token_grad = jnp.sum(
        returned[flat_slot].reshape(tok_rows, top_count, width_part), axis=1
    ).astype(jnp.bfloat16)
    gate_grad = gate_acc.astype(jnp.bfloat16)
    up_grad = up_acc.astype(jnp.bfloat16)
    down_grad = down_acc.astype(jnp.bfloat16)
    return (token_grad, gate_grad, up_grad, down_grad)


def solution(mesh):
    return jax.shard_map(
        shards,
        mesh=mesh,
        in_specs=(
            P("dp", "expert"),
            P("dp", "expert"),
            P("dp", None),
            P("dp", None),
            P(),
            P("dp", "expert", None),
            P("dp", "expert", None),
            P("dp", None, "expert"),
        ),
        out_specs=(
            P("dp", "expert"),
            P("dp", "expert", None),
            P("dp", "expert", None),
            P("dp", None, "expert"),
        ),
        check_vma=False,
    )
```

profile of v0, /device:TPU:32, one launch (start us, length us, event | category | flops | bytes accessed | tf_op | source)
XLA Modules:
  0.0 576.1 jit_solution(13153250661909918266)
XLA Ops:
  12.6 18.0 %reduce-window.6 = s32[64,8,128]{2,1,0:T(8,128)S(1)} reduce-window(s32[64,8,128]{2,1,0:T(8,128)S(1)} %fusion.25, s32[]{:T(128)} %constant.142.clone.1), window={size=1x1x128 pad=0_0x0_0x127_0}, to_apply=%region_0.1 | reduce-window | flops 8323072 | bytes 524292 | tf_op jit(solution)/shard_map/reduce-window
  31.4 6.6 %gather_fusion = s32[1024]{0:T(1024)S(1)} fusion(s32[32]{0:T(128)S(1)} %copy-done.2, s32[1024]{0:T(1024)S(1)} %broadcast_clamp_fusion.1), kind=kCustom, calls=%fused_computation | custom fusion | bytes 12288 | tf_op jit(solution)/shard_map/gather | solution.py:39
  38.4 4.3 scatter_custom_fusion
  43.2 5.4 gather_fusion.2
  48.6 3.6 gather.20
  52.3 5.4 gather_fusion.1
  57.7 3.6 gather.18
  62.0 3.2 copy_select_fusion.1
  65.2 51.2 %all_to_all.15 = bf16[32,24,2,512]{3,1,2,0:T(8,128)(2,1)} all-to-all(bf16[32,24,2,512]{3,1,2,0:T(8,128)(2,1)S(1)} %get-tuple-element.51), channel_id=1, replica_groups=mesh['dp'=32,'expert'=8] {'dp'}, dimensions={0} | all-to-all | bytes 3145728 | tf_op jit(solution)/shard_map/all_to_all | solution.py:64
  116.3 4.9 all-to-all-start.1
  122.2 3.0 collective-permute-start
  127.3 3.1 collective-permute-start.2
  131.6 27.4 %collective-permute-done = bf16[512,768]{1,0:T(8,128)(2,1)} collective-permute-done((bf16[512,768]{1,0:T(8,128)(2,1)}, bf16[512,768]{1,0:T(8,128)(2,1)}, u32[]{:S(2)}, u32[]{:S(2)}) %collective-permute-start) | collective-permute-done | bytes 786464 | tf_op jit(solution)/shard_map/ppermute | solution.py:14
  160.3 16.3 %collective-permute-done.1 = bf16[512,768]{1,0:T(8,128)(2,1)} collective-permute-done((bf16[512,768]{1,0:T(8,128)(2,1)S(1)}, bf16[512,768]{1,0:T(8,128)(2,1)}, u32[]{:S(2)}, u32[]{:S(2)}) %collective-permute-start.1) | collective-permute-done | bytes 786464 | tf_op jit(solution)/shard_map/ppermute | solution.py:14
  178.8 13.3 %collective-permute-done.2 = bf16[768,512]{1,0:T(8,128)(2,1)} collective-permute-done((bf16[768,512]{1,0:T(8,128)(2,1)S(1)}, bf16[768,512]{1,0:T(8,128)(2,1)}, u32[]{:S(2)}, u32[]{:S(2)}) %collective-permute-start.2) | collective-permute-done | bytes 786464 | tf_op jit(solution)/shard_map/ppermute | solution.py:14
  194.5 3.9 convolution_bitcast_fusion.2
  198.4 3.9 convolution_bitcast_fusion.1
  205.0 3.0 convolution_bitcast_fusion
  208.1 5.6 pad_maximum_fusion
  213.6 21.6 %copy.86 = f32[768,2,2304]{2,1,0:T(2,128)} copy(f32[768,2,2304]{0,2,1:T(8,128)} %pad_maximum_fusion) | data formatting | bytes 28311552 | tf_op jit(solution)/shard_map/concatenate | solution.py:74
  237.1 162.2 %all-reduce.3.cloned.1.call-done = f32[768,2,2304]{2,1,0:T(2,128)} async-done(((f32[768,2,2304]{2,1,0:T(2,128)}), f32[768,2,2304]{2,1,0:T(2,128)}) %all-reduce.3.cloned.1.call-update) | async-done | bytes 14155792
  399.4 2.7 constant_dynamic-slice_fusion
  404.4 46.8 %all-gather.2.cloned.1.call-done = bf16[768,2,2304]{2,1,0:T(2,128)(2,1)} async-done(((bf16[96,2,2304]{2,1,0:T(2,128)(2,1)}), bf16[768,2,2304]{2,1,0:T(2,128)(2,1)}) %all-gather.2.cloned.1.call-update) | async-done | bytes 7077904 | tf_op jit(solution)/shard_map/all_gather | solution.py:94
  451.3 8.2 %fusion.35 = (bf16[768,2,768]{2,1,0:T(2,128)(2,1)}, bf16[768,2,768]{2,1,0:T(2,128)(2,1)S(1)}, bf16[768,2,768]{2,1,0:T(2,128)(2,1)S(1)}) fusion(bf16[768,2,2304]{2,1,0:T(2,128)(2,1)} %all-gather.2.cloned.1.call-done), kind=kLoop, calls=%fused_computation.82 | loop fusion | bytes 14155776 | tf_op jit(solution)/shard_map/slice | solution.py:97
  461.6 3.1 add_bitcast_fusion
  469.2 10.2 %all-to-all-start.2 = ((f32[32,24,2,512]{3,1,2,0:T(8,128)}), f32[32,24,2,512]{3,1,2,0:T(8,128)}, u32[]{:S(2)}, u32[]{:S(2)}) async-start(f32[32,24,2,512]{3,1,2,0:T(8,128)} %copy.94), calls=%async_computation.2 | async-start | bytes 6291456 | tf_op jit(solution)/shard_map/all_to_all | solution.py:109
  479.5 4.4 fusion.16
  489.1 62.6 %all-to-all-done.2 = f32[32,24,2,512]{3,1,2,0:T(8,128)} async-done(((f32[32,24,2,512]{3,1,2,0:T(8,128)}), f32[32,24,2,512]{3,1,2,0:T(8,128)}, u32[]{:S(2)}, u32[]{:S(2)}) %all-to-all-start.2) | async-done | bytes 3145760 | tf_op jit(solution)/shard_map/all_to_all | solution.py:109
  551.6 6.1 %copy.95 = f32[32,24,2,512]{3,2,1,0:T(2,128)} copy(f32[32,24,2,512]{3,1,2,0:T(8,128)} %all-to-all-done.2) | data formatting | bytes 6291456 | tf_op jit(solution)/shard_map/all_to_all | solution.py:109
  557.7 3.9 reshape.211
  561.6 4.9 gather_fusion.3
  566.5 2.8 bitcast_reduce_fusion
  (108 shorter events, 35.3 us)
Async XLA Ops:
  7.2 45.1 %copy-start = (bf16[128,512]{1,0:T(8,128)(2,1)S(1)}, bf16[128,512]{1,0:T(8,128)(2,1)}, u32[]{:S(2)}) copy-start(bf16[128,512]{1,0:T(8,128)(2,1)} %param.14) | copy-start | bytes 393220
  7.2 1.9 copy-start.16
  9.1 2.0 copy-start.17
  11.1 1.1 copy-start.19
  12.2 19.1 %copy-start.2 = (s32[32]{0:T(128)S(1)}, s32[32]{0:T(128)}, u32[]{:S(2)}) copy-start(s32[32]{0:T(128)} %param.18) | copy-start | bytes 388
  31.3 11.4 %copy-start.18 = (bf16[128,512]{1,0:T(8,128)(2,1)S(1)}, bf16[128,512]{1,0:T(8,128)(2,1)}, u32[]{:S(2)}) copy-start(bf16[128,512]{1,0:T(8,128)(2,1)} %param.15) | copy-start | bytes 393220
  31.4 11.4 %copy-start.20 = (f32[128,8]{0,1:T(8,128)S(1)}, f32[128,8]{0,1:T(8,128)}, u32[]{:S(2)}) copy-start(f32[128,8]{0,1:T(8,128)} %param.17) | copy-start | bytes 12292
  116.3 85.9 %all-to-all-start.1 = ((bf16[32,24,2,512]{3,1,2,0:T(8,128)(2,1)}), bf16[32,24,2,512]{3,1,2,0:T(8,128)(2,1)}, u32[]{:S(2)}, u32[]{:S(2)}) async-start(bf16[32,24,2,512]{3,1,2,0:T(8,128)(2,1)} %get-tuple-element.52), calls=%async_computation.1 | async-start | bytes 3145728 | tf_op jit(solution)/shard_map/all_to_all | solution.py:65
  121.3 278.1 %all-reduce.3.cloned.1.call-start = ((), (), s32[]{:S(2)}) async-start(), calls=%async_computation.4 | async-start | bytes 28311552
  121.3 3.9 copy-start.6
  122.2 36.7 %collective-permute-start = (bf16[512,768]{1,0:T(8,128)(2,1)}, bf16[512,768]{1,0:T(8,128)(2,1)}, u32[]{:S(2)}, u32[]{:S(2)}) collective-permute-start(bf16[512,768]{1,0:T(8,128)(2,1)} %slice_bitcast_fusion.2), channel_id=1, source_target_pairs={{0,128},{128,0},{8,136},{136,8},{16,144},{144,16},{24,152},{152,24... | collective-permute-start | bytes 2359304 | tf_op jit(solution)/shard_map/ppermute | solution.py:14
  125.3 51.3 %collective-permute-start.1 = (bf16[512,768]{1,0:T(8,128)(2,1)S(1)}, bf16[512,768]{1,0:T(8,128)(2,1)}, u32[]{:S(2)}, u32[]{:S(2)}) collective-permute-start(bf16[512,768]{1,0:T(8,128)(2,1)S(1)} %slice_bitcast_fusion.1), channel_id=1, source_target_pairs={{0,128},{128,0},{8,136},{136,8},{16,144},{144,16},{24,152},{152,24... | collective-permute-start | bytes 2359304 | tf_op jit(solution)/shard_map/ppermute | solution.py:14
  127.3 64.8 %collective-permute-start.2 = (bf16[768,512]{1,0:T(8,128)(2,1)S(1)}, bf16[768,512]{1,0:T(8,128)(2,1)}, u32[]{:S(2)}, u32[]{:S(2)}) collective-permute-start(bf16[768,512]{1,0:T(8,128)(2,1)S(1)} %slice_bitcast_fusion), channel_id=1, source_target_pairs={{0,128},{128,0},{8,136},{136,8},{16,144},{144,16},{24,152},{152,24... | collective-permute-start | bytes 2359304 | tf_op jit(solution)/shard_map/ppermute | solution.py:14
  178.8 15.5 %copy-start.11 = (bf16[32,24,2,512]{3,1,2,0:T(8,128)(2,1)S(1)}, bf16[32,24,2,512]{3,1,2,0:T(8,128)(2,1)}, u32[]{:S(2)}) copy-start(bf16[32,24,2,512]{3,1,2,0:T(8,128)(2,1)} %all_to_all.15) | copy-start | bytes 4718596
  194.4 3.9 copy-start.4
  194.5 3.9 copy-start.7
  202.2 5.8 %slice-start = ((s8[4718592]{0:T(1024)(128)(4,1)}), s8[4194304]{0:T(1024)(128)(4,1)S(1)}, s32[]{:S(2)}) async-start(s8[4718592]{0:T(1024)(128)(4,1)} %bitcast.58), calls=%async_computation.5 | async-start | bytes 8388608
  203.9 1.1 copy-start.12
  205.0 3.0 slice-start.1
  205.0 3.0 copy-start.3
  235.2 0.7 copy-start.21
  235.3 216.0 %all-gather.2.cloned.1.call-start = ((), (), s32[]{:S(2)}) async-start(), calls=%async_computation.3 | async-start | bytes 7962624 | tf_op jit(solution)/shard_map/all_gather | solution.py:94
  451.3 8.2 %copy-start.8 = (bf16[2,512,768]{2,1,0:T(8,128)(2,1)S(1)}, bf16[2,512,768]{2,1,0:T(8,128)(2,1)}, u32[]{:S(2)}) copy-start(bf16[2,512,768]{2,1,0:T(8,128)(2,1)} %bitcast_dynamic-update-slice_fusion.1) | copy-start | bytes 4718596
  459.5 1.4 copy-start.15
  459.5 2.2 copy-start.9
  469.2 10.3 %copy-start.5 = (bf16[32,24,2,512]{3,1,0,2:T(8,128)(2,1)S(1)}, bf16[32,24,2,512]{3,1,0,2:T(8,128)(2,1)}, u32[]{:S(2)}) copy-start(bf16[32,24,2,512]{3,1,0,2:T(8,128)(2,1)} %copy-done.4) | copy-start | bytes 4718596
  469.2 82.4 %all-to-all-start.2 = ((f32[32,24,2,512]{3,1,2,0:T(8,128)}), f32[32,24,2,512]{3,1,2,0:T(8,128)}, u32[]{:S(2)}, u32[]{:S(2)}) async-start(f32[32,24,2,512]{3,1,2,0:T(8,128)} %copy.94), calls=%async_computation.2 | async-start | bytes 6291456 | tf_op jit(solution)/shard_map/all_to_all | solution.py:109
  479.5 4.4 copy-start.10
  483.9 2.6 copy-start.13
  483.9 2.6 copy-start.14
  561.6 7.7 %copy-start.1 = (bf16[128,512]{1,0:T(8,128)(2,1)S(1)}, bf16[128,512]{1,0:T(8,128)(2,1)}, u32[]{:S(2)}) copy-start(bf16[128,512]{1,0:T(8,128)(2,1)} %param.14) | copy-start | bytes 393220
Sparse Core Ops, SparseCore 0:
  235.4 163.9 all-reduce.2
  404.5 46.6 all-gather.1
where the time goes:
time: 580 us; the launch traced here: 576 us
  waiting for transfers between devices  329 us (57%)
  local copies, waits for them, and re-layouts  97 us (17%)
  blocking collectives  51.2 us (9%)
  other arithmetic  36.5 us (6%)
  matrix products  24.8 us (4%)
  starting transfers between devices  22.3 us (4%)
  between operations  15.8 us (3%)
    unnamed x3, waiting for transfers between devices  162 us
    all_to_all x1, waiting for transfers between devices, shards(): lax.all_to_all(rows_acc.reshape(dp_size, most_rows, per_host, width_part)...  62.6 us
    ppermute x3, waiting for transfers between devices, from_partner(): return lax.ppermute(block, axis, route)  56.9 us
    all_to_all x1, blocking collectives, shards(): lax.all_to_all(token_send, 'dp', split_axis=0, concat_axis=0, tiled=True)  51.2 us
    all_gather x1, waiting for transfers between devices, shards(): piece = lax.all_gather(acts, 'expert', axis=0, tiled=True)  46.8 us
    concatenate x1, local copies, waits for them, and re-layouts, shards(): jnp.concatenate([jnp.concatenate([gate_pre, up_pre], axis=2), jnp.einsum(...  21.6 us
    another operation x4, other arithmetic  18.6 us
  transfers between devices with their start and end apart: 7, of which 6 were waited for; matrix products, arithmetic and copies ran while one was open for 5% of the time, Pallas kernels for 0%

commit v1 on v0

v1 whole, which is shorter than its diff:
```python
import functools

import jax
import jax.numpy as jnp
from jax import lax
from jax.experimental import pallas as pl
from jax.experimental.pallas import tpu as pltpu
from jax.sharding import PartitionSpec as P

BF = jnp.bfloat16
F32 = jnp.float32
MESH = pl.DeviceIdType.MESH
NX, NZ, NY = 4, 8, 4
FF = 768


def dot(a, b):
    return lax.dot_general(a, b, (((1,), (0,)), ((), ())), preferred_element_type=F32)


def dot_nt(a, b):
    return lax.dot_general(a, b, (((1,), (1,)), ((), ())), preferred_element_type=F32)


def dot_tn(a, b):
    return lax.dot_general(a, b, (((0,), (0,)), ((), ())), preferred_element_type=F32)


def kernel(
    plan, tok, cot, meta, wg, wu, wd,
    tg_o, gg_o, ug_o, dg_o,
    T, C, M, X, G, RK, GV, RK2, CS, CR, H, SY, RY, PS, PR, AB0, ABA, ABB, R, RB, DS, ZR,
    ax_s, ax_r, az_s, az_r, bz_s, bz_r, bx_s, bx_r, cs_s, cs_r, sy_s, sy_r,
    ps_s, ps_r, ag_s, ag_r, rx_s, rx_r, rz_s, rz_r,
):
    dp = lax.axis_index("dp")
    ex = lax.axis_index("expert")
    x, z = lax.div(dp, NZ), lax.rem(dp, NZ)
    y, c = lax.div(ex, 2), lax.rem(ex, 2)

    def at(xx, zz):
        return lax.rem(xx, NX) * NZ + lax.rem(zz, NZ)

    def yc(yy, cc):
        return lax.rem(yy, NY) * 2 + cc

    peer = (dp, yc(y, 1 - c))
    up_y, down_y = (dp, yc(y + 1, c)), (dp, yc(y + 3, c))
    x_to = [None] + [(at(x + j, z), ex) for j in (1, 2, 3)]
    z_to = [None] + [(at(x, z + i), ex) for i in range(1, NZ)]

    barrier = pltpu.get_barrier_semaphore()
    others = [peer, up_y, down_y] + x_to[1:] + z_to[1:]
    for other in others:
        pl.semaphore_signal(barrier, inc=1, device_id=other, device_id_type=MESH)
    pl.semaphore_wait(barrier, len(others))

    sent = []

    def go(src, dst, s, r, to):
        copy = pltpu.make_async_remote_copy(
            src_ref=src, dst_ref=dst, send_sem=s, recv_sem=r, device_id=to, device_id_type=MESH
        )
        copy.start()
        sent.append(copy)
        return copy

    ax, az, bz, bx = {}, {}, {}, {}

    def send_az(way, j, h):
        for a, buf in enumerate((T, M)):
            b = at(x + 4 - j, z + (8 - (h - 1) if way == 0 else h - 1))
            src = buf.at[b] if (j or h > 1) else (tok, meta)[a]
            az[way, a, j, h] = go(
                src, buf.at[b], az_s.at[way, a, j, h - 1], az_r.at[way, a, j, h - 1],
                z_to[1] if way == 0 else z_to[7],
            )

    def send_bz(way, h):
        b = at(x, z + (8 - (h - 1) if way == 0 else h - 1))
        src = C.at[b] if h > 1 else cot
        bz[way, h] = go(
            src, C.at[b], bz_s.at[way, h - 1], bz_r.at[way, h - 1], z_to[1] if way == 0 else z_to[7]
        )

    def send_bx(d):
        b = at(x, z + d)
        for j in (1, 2, 3):
            bx[j, d] = go(
                C.at[b] if d else cot, C.at[b], bx_s.at[j - 1, d], bx_r.at[j - 1, d], x_to[j]
            )

    for j in (1, 2, 3):
        for a, (buf, src) in enumerate(((T, tok), (M, meta))):
            ax[a, j] = go(src, buf.at[dp], ax_s.at[a, j - 1], ax_r.at[a, j - 1], x_to[j])
    send_bz(0, 1)
    send_bz(1, 1)
    send_az(0, 0, 1)
    send_az(1, 0, 1)
    send_bx(0)
    T[dp] = tok[...]
    C[dp] = cot[...]
    M[dp] = meta[...]
    last = lambda way, j: 4 if (j + way) % 2 == 0 else 3
    for j in (1, 2, 3):
        for a in (0, 1):
            ax[a, j].wait_recv()
        send_az(0, j, 1)
        send_az(1, j, 1)
    for h in (1, 2, 3, 4):
        for way in (0, 1):
            if h <= 4 - way:
                bz[way, h].wait_recv()
                if h < 4 - way:
                    send_bz(way, h + 1)
                send_bx(8 - h if way == 0 else h)
        for j in range(4):
            for way in (0, 1):
                if h <= last(way, j):
                    for a in (0, 1):
                        az[way, a, j, h].wait_recv()
                    if h < last(way, j):
                        send_az(way, j, h + 1)

    flag = jnp.full((1, 128), plan[dp].astype(F32))
    far = lax.rem(dp + NX * NZ // 2, NX * NZ)
    own_id = (2 * dp + 1).astype(F32)
    star_id = flag * (2 * far + 1).astype(F32) + (1.0 - flag) * own_id
    row_i = lax.broadcasted_iota(jnp.int32, (128, 128), 0)
    col_i = lax.broadcasted_iota(jnp.int32, (128, 128), 1)
    upper = jnp.where(row_i <= col_i, 1.0, 0.0).astype(BF)

    def places(ids, target):
        match = ids == target
        hit = jnp.sum(jnp.where(match, 1.0, 0.0), axis=1)
        return match, jnp.where(hit > 0.0, dot(hit.astype(BF), upper) - 1.0, -1000.0)

    ids, gates = M[:, 0:8, :], M[:, 8:16, :]
    for i, target in enumerate(((2 * dp).astype(F32), own_id, star_id[:, None, :])):
        match, rank = places(ids, target)
        RK[i] = rank
        GV[i] = jnp.sum(jnp.where(match, gates, 0.0), axis=1)
    near = M[pl.ds(pl.multiple_of(x * NZ, NZ), NZ), 0:8, :]
    for e in (0, 1):
        for j in range(4):
            _, rank = places(near, (2 * at(x + 4 - j, z) + e).astype(F32))
            RK2[e * 4 + j] = rank

    for j in (1, 2, 3):
        for d in range(8):
            bx[j, d].wait_recv()

    slot_i = lax.broadcasted_iota(jnp.int32, (48, 256), 0).astype(F32)

    def pick(q, carry):
        ones, scale = [], []
        for i in range(3):
            r0 = RK[i, pl.ds(2 * q, 1), :]
            r1 = RK[i, pl.ds(2 * q + 1, 1), :] + 24.0
            eq = slot_i == jnp.concatenate([r0, r1], axis=1)
            g = jnp.concatenate([GV[i, pl.ds(2 * q, 1), :], GV[i, pl.ds(2 * q + 1, 1), :]], axis=1)
            ones.append(jnp.where(eq, 1.0, 0.0).astype(BF))
            scale.append(jnp.sum(jnp.where(eq, g, 0.0), axis=1, keepdims=True))
        ones = jnp.concatenate(ones, axis=0)
        scale = jnp.concatenate(scale, axis=0)
        xs = dot(ones, T[pl.ds(2 * q, 2)].reshape(256, 512)).astype(BF)
        gs = (dot(ones, C[pl.ds(2 * q, 2)].reshape(256, 512)) * scale).astype(BF)
        at_row = pl.ds(pl.multiple_of(48 * q, 16), 48)
        for i in range(3):
            X[i, at_row, :] = xs[48 * i : 48 * i + 48]
            G[i, at_row, :] = gs[48 * i : 48 * i + 48]
        return carry

    lax.fori_loop(0, 16, pick, 0)

    cs = {}

    def project(e, mine):
        rows = pl.ds(pl.multiple_of((c if mine else 1 - c) * 384, 384), 384)
        xs, gs = X[e, rows, :], G[e, rows, :]
        for n in range(9):
            t = slice(n % 3 * 256, n % 3 * 256 + 256)
            if n < 3:
                res = dot(xs, wg[e, :, t])
            elif n < 6:
                res = dot(xs, wu[e, :, t])
            else:
                res = dot_nt(gs, wd[e, t, :])
            if mine:
                H[e, :, n * 256 : n * 256 + 256] = res
            else:
                CS[e, :, n * 256 : n * 256 + 256] = res.astype(BF)
        if not mine:
            cs[e] = go(CS.at[e], CR.at[e], cs_s.at[e], cs_r.at[e], peer)

    sy = {}

    def part(e, yy, off, col):
        rows = pl.ds(pl.multiple_of(lax.rem(yy, NY) * 96 + off, 16), 48)
        return H[e, rows, col] + CR[e, rows, col].astype(F32)

    def tiles(body, n=9, width=256):
        def step(i, carry):
            body(pl.ds(pl.multiple_of(i * width, width), width))
            return carry

        lax.fori_loop(0, n, step, 0)

    def message(e, m, yy, off, plus=None):
        def body(col):
            v = part(e, yy, off, col)
            if plus is not None:
                v = v + RY[e, plus, :, col].astype(F32)
            SY[e, m, :, col] = v.astype(BF)

        tiles(body)
        sy[e, m] = go(
            SY.at[e, m], RY.at[e, m], sy_s.at[e, m], sy_r.at[e, m], up_y if m in (0, 1, 4) else down_y
        )

    def ring_one(e):
        cs[e].wait_recv()
        message(e, 0, y + 2, 0)
        message(e, 2, y + 2, 48)
        message(e, 1, y + 1, 48)
        message(e, 3, y + 3, 0)

    def ring_two(e):
        sy[e, 0].wait_recv()
        message(e, 4, y + 1, 0, plus=0)
        sy[e, 2].wait_recv()
        message(e, 5, y + 3, 48, plus=2)

    mine = c * 4 + y

    def activate(e):
        for m in (1, 3, 4, 5):
            sy[e, m].wait_recv()
        for rr in (0, 1):
            rows = slice(rr * 48, rr * 48 + 48)
            a, b = ((4, 3), (5, 1))[rr]

            def body(i, carry):
                def total(kind):
                    col = pl.ds(pl.multiple_of(kind * FF + i * 128, 128), 128)
                    v = part(e, y, rr * 48, col)
                    return v + RY[e, a, :, col].astype(F32) + RY[e, b, :, col].astype(F32)

                gate, up, back = total(0), total(1), total(2)
                sig = jax.nn.sigmoid(gate)
                silu = gate * sig
                hid = (silu * up).astype(BF)
                gd = (back * up * sig * (1.0 + gate * (1.0 - sig))).astype(BF)
                ud = (back * silu).astype(BF)
                cols = [pl.ds(pl.multiple_of(k * FF + i * 128, 128), 128) for k in range(3)]
                if e == 0:
                    for k, v in enumerate((hid, gd, ud)):
                        AB0[mine, rows, cols[k]] = v
                else:
                    for k, v in enumerate((hid, gd, ud)):
                        PS[rows, cols[k]] = v
                    ABA[mine, rows, cols[0]] = gd
                    ABA[mine, rows, cols[1]] = ud
                return carry

            lax.fori_loop(0, 6, body, 0)

    ag = {}
    ABS = (ABA, ABB, AB0)

    def ag_own(i):
        own = ABS[i].at[mine]
        for n, to in ((0, up_y), (1, down_y), (2, peer)):
            ag[i, n] = go(own, own, ag_s.at[i, n], ag_r.at[i, n], to)

    def ag_pass(i):
        for n, (yy, off, to) in enumerate(((y + 3, 0, up_y), (y + 1, 48, down_y))):
            ag[i, n].wait_recv()
            k = c * 4 + lax.rem(yy, NY)
            part_ref = ABS[i].at[k, pl.ds(off, 48)]
            ag[i, 3 + n] = go(part_ref, part_ref, ag_s.at[i, 3 + n], ag_r.at[i, 3 + n], to)
            whole = ABS[i].at[k]
            ag[i, 5 + n] = go(whole, whole, ag_s.at[i, 5 + n], ag_r.at[i, 5 + n], peer)

    def ag_end(i):
        ag[i, 3].wait_recv()
        ag[i, 4].wait_recv()
        whole = ABS[i].at[c * 4 + lax.rem(y + 2, NY)]
        ag[i, 7] = go(whole, whole, ag_s.at[i, 7], ag_r.at[i, 7], peer)

    def ag_done(i):
        for n in (2, 5, 6, 7):
            ag[i, n].wait_recv()

    rx = {}

    def back_rows(e):
        ab, g0 = (AB0, FF) if e == 0 else (ABA, 0)

        def step(i, carry):
            k = pl.ds(pl.multiple_of(i * 4, 4), 4)
            gd = ab[k, :, g0 : g0 + FF].reshape(384, FF)
            ud = ab[k, :, g0 + FF : g0 + 2 * FF].reshape(384, FF)
            for n in (0, 256):
                res = dot_nt(gd, wg[e, n : n + 256, :]) + dot_nt(ud, wu[e, n : n + 256, :])
                R[e, pl.ds(pl.multiple_of(i * 8, 8), 8), :, n : n + 256] = res.astype(BF).reshape(8, 48, 256)
            return carry

        lax.fori_loop(0, 2, step, 0)
        for j in (1, 2, 3):
            q = pl.ds(pl.multiple_of(lax.rem(x + j, NX) * 4, 4), 4)
            rx[e, j] = go(
                R.at[e, q], RB.at[:, e * 4 + j], rx_s.at[e, j - 1], rx_r.at[e, j - 1], x_to[j]
            )
        RB[:, e * 4] = R[e, pl.ds(pl.multiple_of(x * 4, 4), 4)]

    def weight_grads(slot, ab, h0, i):
        def inputs(n, carry):
            d = pl.ds(pl.multiple_of(n * 256, 256), 256)
            xs = X[i, :, d]
            for k, out in ((1, gg_o), (2, ug_o)):
                act = ab[:, :, h0 + k * FF : h0 + (k + 1) * FF].reshape(FF, FF)
                out[slot, d, :] = dot_tn(xs, act).astype(BF)
            return carry

        lax.fori_loop(0, 2, inputs, 0)

        def hidden(n, carry):
            f = pl.ds(pl.multiple_of(n * 256, 256), 256)
            hid = ab[:, :, pl.ds(pl.multiple_of(h0 + n * 256, 256), 256)].reshape(FF, 256)
            dg_o[slot, f, :] = dot_tn(hid, G[i]).astype(BF)
            return carry

        lax.fori_loop(0, 3, hidden, 0)

    project(1, False)
    project(1, True)
    ring_one(1)
    project(0, False)
    project(0, True)
    ring_two(1)
    ring_one(0)
    activate(1)
    swap = go(PS, PR, ps_s.at[0], ps_r.at[0], x_to[2])
    ag_own(0)
    ring_two(0)
    ag_pass(0)
    swap.wait_recv()

    def choose(col):
        keep = jnp.full((96, 256), plan[dp].astype(F32)) > 0.5
        v = jnp.where(keep, PR[:, col].astype(F32), PS[:, col].astype(F32))
        ABB[mine, :, col] = v.astype(BF)

    tiles(choose)
    ag_own(1)
    activate(0)
    ag_own(2)
    ag_end(0)
    ag_pass(1)
    ag_done(0)
    back_rows(1)
    ag_end(1)
    ag_pass(2)
    ag_done(1)
    weight_grads(1, ABB, 0, 2)
    ag_end(2)
    ag_done(2)
    back_rows(0)

    for e in (1, 0):
        for j in (1, 2, 3):
            rx[e, j].wait_recv()

    def dense(p):
        pieces = []
        for s in range(8):
            r0 = RK2[s, pl.ds(2 * p, 1), :]
            r1 = RK2[s, pl.ds(2 * p + 1, 1), :] + 24.0
            pieces.append(
                jnp.where(slot_i == jnp.concatenate([r0, r1], axis=1), 1.0, 0.0).astype(BF)
            )
        return dot_tn(jnp.concatenate(pieces, axis=0), RB[p].reshape(384, 512))

    def rz_copy(zt):
        return pltpu.make_async_remote_copy(
            src_ref=DS.at[zt], dst_ref=ZR.at[z], send_sem=rz_s.at[zt], recv_sem=rz_r.at[z],
            device_id=(at(x, zt), ex), device_id_type=MESH,
        )

    half = lax.div(z, 2)

    def spread(i, carry):
        p = lax.rem(half + 1 + i, 4)
        v = dense(p)
        DS[pl.ds(2 * p, 2)] = v.astype(BF).reshape(2, 128, 512)
        rz_copy(2 * p).start()
        rz_copy(2 * p + 1).start()
        return carry

    lax.fori_loop(0, 3, spread, 0)
    v = dense(half)
    DS[pl.ds(2 * half, 2)] = v.astype(BF).reshape(2, 128, 512)
    mate = 2 * half + 1 - lax.rem(z, 2)
    rz_copy(mate).start()

    weight_grads(0, AB0, 0, 0)

    total = DS[z].astype(F32)
    for i in range(1, 8):
        zs = lax.rem(z + i, NZ)
        pltpu.make_async_remote_copy(
            src_ref=DS.at[zs], dst_ref=ZR.at[zs], send_sem=rz_s.at[zs], recv_sem=rz_r.at[zs],
            device_id=(at(x, zs), ex), device_id_type=MESH,
        ).wait()
        total = total + ZR[zs].astype(F32)
    tg_o[...] = total.astype(BF)
    for copy in sent:
        copy.wait_send()


def shards(tokens, cotangent, expert_ids, gate_values, swap_plan, gate_weight, up_weight, down_weight):
    meta = jnp.concatenate([expert_ids.T.astype(F32), gate_values.T], axis=0)
    vmem = pl.BlockSpec(memory_space=pltpu.VMEM)
    dma = lambda *shape: [pltpu.SemaphoreType.DMA(shape), pltpu.SemaphoreType.DMA(shape)]
    w = 3 * FF
    return pl.pallas_call(
        kernel,
        out_shape=(
            jax.ShapeDtypeStruct(tokens.shape, BF),
            jax.ShapeDtypeStruct(gate_weight.shape, BF),
            jax.ShapeDtypeStruct(up_weight.shape, BF),
            jax.ShapeDtypeStruct(down_weight.shape, BF),
        ),
        in_specs=[pl.BlockSpec(memory_space=pltpu.SMEM)] + [vmem] * 6,
        out_specs=(vmem,) * 4,
        scratch_shapes=[
            pltpu.VMEM((32, 128, 512), BF),
            pltpu.VMEM((32, 128, 512), BF),
            pltpu.VMEM((32, 16, 128), F32),
            pltpu.VMEM((3, 768, 512), BF),
            pltpu.VMEM((3, 768, 512), BF),
            pltpu.VMEM((3, 32, 128), F32),
            pltpu.VMEM((3, 32, 128), F32),
            pltpu.VMEM((8, 8, 128), F32),
            pltpu.VMEM((2, 384, w), BF),
            pltpu.VMEM((2, 384, w), BF),
            pltpu.VMEM((2, 384, w), F32),
            pltpu.VMEM((2, 6, 48, w), BF),
            pltpu.VMEM((2, 6, 48, w), BF),
            pltpu.VMEM((96, w), BF),
            pltpu.VMEM((96, w), BF),
            pltpu.VMEM((8, 96, w), BF),
            pltpu.VMEM((8, 96, 2 * FF), BF),
            pltpu.VMEM((8, 96, w), BF),
            pltpu.VMEM((2, 16, 48, 512), BF),
            pltpu.VMEM((4, 8, 48, 512), BF),
            pltpu.VMEM((8, 128, 512), BF),
            pltpu.VMEM((8, 128, 512), BF),
        ]
        + dma(2, 3)
        + dma(2, 2, 4, 4)
        + dma(2, 4)
        + dma(3, 8)
        + dma(2)
        + dma(2, 6)
        + dma(1)
        + dma(3, 8)
        + dma(2, 3)
        + dma(8),
        compiler_params=pltpu.CompilerParams(
            collective_id=0, has_side_effects=True, vmem_limit_bytes=62 << 20
        ),
        cost_estimate=pl.CostEstimate(flops=10_000_000_000, bytes_accessed=10_000_000, transcendentals=0),
        name="expert_layer",
    )(swap_plan, tokens, cotangent, meta, gate_weight, up_weight, down_weight)


def solution(mesh):
    return jax.shard_map(
        shards,
        mesh=mesh,
        in_specs=(
            P("dp", "expert"),
            P("dp", "expert"),
            P("dp", None),
            P("dp", None),
            P(),
            P("dp", "expert", None),
            P("dp", "expert", None),
            P("dp", None, "expert"),
        ),
        out_specs=(
            P("dp", "expert"),
            P("dp", "expert", None),
            P("dp", "expert", None),
            P("dp", None, "expert"),
        ),
        check_vma=False,
    )
```

time: 580 us -> 201 us (0.35)
  waiting for transfers between devices: 329 us -> 0 us
  Pallas kernels: 0 us -> 189 us
  local copies, waits for them, and re-layouts: 97 us -> 7.46 us
  blocking collectives: 51.2 us -> 0 us
  other arithmetic: 36.5 us -> 1.98 us
  matrix products: 24.8 us -> 0 us
  starting transfers between devices: 22.3 us -> 0 us
  between operations: 15.8 us -> 0.64 us
    pallas_call x0 -> x1, Pallas kernels: none -> 189 us  [shards(): pl.pallas_call(kernel, out_shape=(jax.ShapeDtypeStruct(tokens.shape, BF),...]
    unnamed x3 -> x0, waiting for transfers between devices: 162 us -> none
    all_to_all x2 -> x0, waiting for transfers between devices: 62.6 us -> none  [the longest x1 62.6 us: shards(): lax.all_to_all(rows_acc.reshape(dp_size, most_rows, per_host, width_part)...]
    ppermute x3 -> x0, waiting for transfers between devices: 56.9 us -> none  [from_partner(): return lax.ppermute(block, axis, route)]
    all_to_all x1 -> x0, blocking collectives: 51.2 us -> none  [shards(): lax.all_to_all(token_send, 'dp', split_axis=0, concat_axis=0, tiled=True)]
    all_gather x1 -> x0, waiting for transfers between devices: 46.8 us -> none  [shards(): piece = lax.all_gather(acts, 'expert', axis=0, tiled=True)]
    gather x6 -> x0, local copies, waits for them, and re-layouts: 29.5 us -> none  [the longest x2 9.04 us: shards(): tokens[source // top_count]]
    dot_general x8 -> x0, matrix products: 24.8 us -> none  [the longest x1 4.4 us: shards(): jnp.einsum('rsd,rsf->sdf', x_part, up_part, preferred_element_type=jnp.fl...]
  transfers between devices with their start and end apart: 7 -> 0, of which waited for: 6 -> 0; matrix products, arithmetic and copies ran while one was open for 5% -> 0% of each run, Pallas kernels for 0% -> 0%
where the time goes in v1:
time: 201 us; the launch traced here: 199 us
  Pallas kernels  189 us (94%)
  local copies, waits for them, and re-layouts  7.46 us (4%)
    pallas_call x1, Pallas kernels, shards(): pl.pallas_call(kernel, out_shape=(jax.ShapeDtypeStruct(tokens.shape, BF),...  189 us
    unnamed x8, local copies, waits for them, and re-layouts  7.46 us

profile of v1, /device:TPU:32, one launch (start us, length us, event | category | flops | bytes accessed | tf_op | source)
XLA Modules:
  0.0 199.3 jit_solution(14555123691951833072)
XLA Ops:
  0.6 0.7 convert_bitcast_fusion
  1.3 1.3 pad_maximum_fusion.meta
  2.6 189.2 %expert_layer.1 = (bf16[128,512]{1,0:T(8,128)(2,1)}, bf16[2,512,768]{2,1,0:T(8,128)(2,1)}, bf16[2,512,768]{2,1,0:T(8,128)(2,1)}, bf16[2,768,512]{2,1,0:T(8,128)(2,1)}) custom-call(s32[32]{0:T(128)} %plan.1, bf16[128,512]{1,0:T(8,128)(2,1)} %tok.1, bf16[128,512]{1,0:T(8,128)(2,1)} %cot.1, f32[16,128]{1,0:T(8,128)} %pad_maximum_fusion.meta, ...), custom_call_target="tpu_custom_call" | custom-call | flops 10000000000 | bytes 10000000 | tf_op jit(solution)/shard_map/expert_layer/pallas_call | solution.py:427
  191.8 1.6 copy.16
  193.4 0.0 copy-start.1
  193.4 2.8 %copy.17 = bf16[2,512,768]{2,1,0:T(8,128)(2,1)} copy(bf16[2,512,768]{2,1,0:T(8,128)(2,1)} %get-tuple-element.9) | data formatting | bytes 3145728
  196.1 0.0 copy-done.1
  196.1 0.0 copy-start
  196.1 1.1 copy.18
  197.3 0.8 copy-done
  198.1 1.1 copy.19
Async XLA Ops:
  193.4 2.8 %copy-start.1 = (bf16[2,512,768]{2,1,0:T(8,128)(2,1)S(1)}, bf16[2,512,768]{2,1,0:T(8,128)(2,1)}, u32[]{:S(2)}) copy-start(bf16[2,512,768]{2,1,0:T(8,128)(2,1)} %get-tuple-element.10) | copy-start | bytes 4718596
  196.1 2.0 copy-start

commit v2 on v0

v2 whole, which is shorter than its diff:
```python
import functools

import jax
import jax.numpy as jnp
from jax import lax
from jax.experimental import pallas as pl
from jax.experimental.pallas import tpu as pltpu
from jax.sharding import PartitionSpec as P

BF = jnp.bfloat16
F32 = jnp.float32
MESH = pl.DeviceIdType.MESH
NX, NZ, NY = 4, 8, 4
FF = 768


def dot(a, b):
    return lax.dot_general(a, b, (((1,), (0,)), ((), ())), preferred_element_type=F32)


def dot_nt(a, b):
    return lax.dot_general(a, b, (((1,), (1,)), ((), ())), preferred_element_type=F32)


def dot_tn(a, b):
    return lax.dot_general(a, b, (((0,), (0,)), ((), ())), preferred_element_type=F32)


def kernel(
    plan, tok, cot, ids_in, gates_in, wg, wu, wd,
    tg_o, gg_o, ug_o, dg_o,
    T, C, M, X, G, RK, GV, RK2, CS, CR, H, SY, RY, PS, PR, AB, AH, R, RB, DS, ZR, OWN,
    mx_s, mx_r, mz_s, mz_r, ax_s, ax_r, az_s, az_r, bz_s, bz_r, bx_s, bx_r, cs_s, cs_r,
    sy_s, sy_r, ps_s, ps_r, ag_s, ag_r, ah_s, ah_r, rx_s, rx_r, rz_s, rz_r,
):
    dp = lax.axis_index("dp")
    ex = lax.axis_index("expert")
    x, z = lax.div(dp, NZ), lax.rem(dp, NZ)
    y, c = lax.div(ex, 2), lax.rem(ex, 2)
    other = 1 - c

    def at(xx, zz):
        return lax.rem(xx, NX) * NZ + lax.rem(zz, NZ)

    turn = 1 + 2 * c
    y_a, y_b, y_opp = lax.rem(y + turn, NY), lax.rem(y + NY - turn, NY), lax.rem(y + 2, NY)
    peer = (dp, y * 2 + other)
    to_a, to_b = (dp, y_a * 2 + c), (dp, y_b * 2 + c)
    x_to = [None] + [(at(x + j, z), ex) for j in (1, 2, 3)]
    z_to = [None] + [(at(x, z + i), ex) for i in range(1, NZ)]

    barrier = pltpu.get_barrier_semaphore()
    group = [peer, to_a, to_b] + x_to[1:] + z_to[1:]
    for device in group:
        pl.semaphore_signal(barrier, inc=1, device_id=device, device_id_type=MESH)
    pl.semaphore_wait(barrier, len(group))

    def rc(src, dst, s, r, to):
        return pltpu.make_async_remote_copy(
            src_ref=src, dst_ref=dst, send_sem=s, recv_sem=r, device_id=to, device_id_type=MESH
        )

    sent = []

    def go(*how):
        copy = rc(*how)
        copy.start()
        sent.append(copy)
        return copy

    mx, mz, ax, az, bz, bx = {}, {}, {}, {}, {}, {}

    def send_az(way, j, h):
        b = at(x + 4 - j, z + (8 - (h - 1) if way == 0 else h - 1))
        az[way, j, h] = go(
            T.at[b] if (j or h > 1) else tok, T.at[b], az_s.at[way, j, h - 1], az_r.at[way, j, h - 1],
            z_to[1] if way == 0 else z_to[7],
        )

    def send_bz(way, h):
        b = at(x, z + (8 - (h - 1) if way == 0 else h - 1))
        bz[way, h] = go(
            C.at[b] if h > 1 else cot, C.at[b], bz_s.at[way, h - 1], bz_r.at[way, h - 1],
            z_to[1] if way == 0 else z_to[7],
        )

    def send_bx(d):
        b = at(x, z + d)
        for j in (1, 2, 3):
            bx[j, d] = go(
                C.at[b] if d else cot, C.at[b], bx_s.at[j - 1, d], bx_r.at[j - 1, d], x_to[j]
            )

    def last(way, j):
        return 4 if (j + way) % 2 == 0 else 3

    M[z, x, 0:8, :] = ids_in[...].astype(F32)
    M[z, x, 8:16, :] = gates_in[...]
    for j in (1, 2, 3):
        mx[j] = go(M.at[z, x], M.at[z, x], mx_s.at[j - 1], mx_r.at[j - 1], x_to[j])
    for j in (1, 2, 3):
        ax[j] = go(tok, T.at[dp], ax_s.at[j - 1], ax_r.at[j - 1], x_to[j])
    send_bz(0, 1)
    send_bz(1, 1)
    send_bx(0)
    for j in (1, 2, 3):
        mx[j].wait_recv()
    for i in range(1, NZ):
        mz[i] = go(M.at[z], M.at[z], mz_s.at[i], mz_r.at[i], z_to[i])
    send_az(0, 0, 1)
    send_az(1, 0, 1)
    T[dp] = tok[...]
    C[dp] = cot[...]
    for j in (1, 2, 3):
        ax[j].wait_recv()
        send_az(0, j, 1)
        send_az(1, j, 1)

    def hop(h):
        for way in (0, 1):
            if h <= 4 - way:
                bz[way, h].wait_recv()
                if h < 4 - way:
                    send_bz(way, h + 1)
                send_bx(8 - h if way == 0 else h)
        for j in range(4):
            for way in (0, 1):
                if h <= last(way, j):
                    az[way, j, h].wait_recv()
                    if h < last(way, j):
                        send_az(way, j, h + 1)

    def all_places():
        for i in range(1, NZ):
            mz[i].wait_recv()
        flag = jnp.full((1, 128), plan[dp].astype(F32))
        far = lax.rem(dp + NX * NZ // 2, NX * NZ)
        own_id = (2 * dp + 1).astype(F32)
        star_id = flag * (2 * far + 1).astype(F32) + (1.0 - flag) * own_id
        row_i = lax.broadcasted_iota(jnp.int32, (128, 128), 0)
        col_i = lax.broadcasted_iota(jnp.int32, (128, 128), 1)
        upper = jnp.where(row_i <= col_i, 1.0, 0.0).astype(BF)

        def places(ids, target):
            match = ids == target
            hit = jnp.sum(jnp.where(match, 1.0, 0.0), axis=1)
            return match, jnp.where(hit > 0.0, dot(hit.astype(BF), upper) - 1.0, -1000.0)

        ids = M[:, :, 0:8, :].reshape(32, 8, 128)
        gates = M[:, :, 8:16, :].reshape(32, 8, 128)
        for i, target in enumerate(((2 * dp).astype(F32), own_id, star_id[:, None, :])):
            match, rank = places(ids, target)
            RK[i] = rank
            GV[i] = jnp.sum(jnp.where(match, gates, 0.0), axis=1)
        near = M[:, pl.ds(x, 1), 0:8, :].reshape(8, 8, 128)
        for j in range(4):
            for e in (0, 1):
                _, rank = places(near, (2 * at(x + 4 - j, z) + e).astype(F32))
                RK2[j * 2 + e] = rank

    slot_i = lax.broadcasted_iota(jnp.int32, (48, 256), 0).astype(F32)

    def tiles(body, n=9, width=256):
        def step(i, carry):
            body(pl.ds(pl.multiple_of(i * width, width), width))
            return carry

        lax.fori_loop(0, n, step, 0)

    def pick(ch):
        for d in {(8 - ch) % 8, ch + 1}:
            for j in (1, 2, 3):
                bx[j, d].wait_recv()

        def step(j, carry):
            ba, bb = at(j, z + 8 - ch), at(j, z + 1 + ch)
            ra = lax.rem(z + 8 - ch, NZ) * 4 + j
            rb = lax.rem(z + 1 + ch, NZ) * 4 + j
            ones, scale = [], []
            for i in range(3):
                r0 = RK[i, pl.ds(ra, 1), :]
                r1 = RK[i, pl.ds(rb, 1), :] + 24.0
                eq = slot_i == jnp.concatenate([r0, r1], axis=1)
                g = jnp.concatenate([GV[i, pl.ds(ra, 1), :], GV[i, pl.ds(rb, 1), :]], axis=1)
                ones.append(jnp.where(eq, 1.0, 0.0).astype(BF))
                scale.append(jnp.sum(jnp.where(eq, g, 0.0), axis=1, keepdims=True))
            ones = jnp.concatenate(ones, axis=0)
            scale = jnp.concatenate(scale, axis=0)
            xs = dot(ones, jnp.concatenate([T[ba], T[bb]], axis=0)).astype(BF)
            gs = (dot(ones, jnp.concatenate([C[ba], C[bb]], axis=0)) * scale).astype(BF)
            rows = pl.ds(pl.multiple_of(48 * j, 16), 48)
            for i in range(3):
                X[i, ch, rows, :] = xs[48 * i : 48 * i + 48]
                G[i, ch, rows, :] = gs[48 * i : 48 * i + 48]
            return carry

        lax.fori_loop(0, 4, step, 0)

    cs, sy = {}, {}

    def project(ch):
        for own in (False, True):
            e = c if own else other
            for kind, w in enumerate((wg, wu, wd)):
                for n in range(0, FF, 256):
                    if kind < 2:
                        res = dot(X[e, ch], w[e, :, n : n + 256])
                    else:
                        res = dot_nt(G[e, ch], w[e, n : n + 256, :])
                    col = slice(kind * FF + n, kind * FF + n + 256)
                    if own:
                        H[ch % 2, :, col] = res
                    else:
                        CS[ch, :, col] = res.astype(BF)
            if not own:
                cs[ch] = go(CS.at[ch], CR.at[ch], cs_s.at[ch], cs_r.at[ch], peer)

    def part(ch, yy, col):
        rows = pl.ds(pl.multiple_of(yy * 48, 16), 48)
        return H[ch % 2, rows, col] + CR[ch, rows, col].astype(F32)

    def message(ch, m, yy, to, plus=None):
        def body(col):
            v = part(ch, yy, col)
            if plus is not None:
                v = v + RY[ch, plus, :, col].astype(F32)
            SY[ch, m, :, col] = v.astype(BF)

        tiles(body)
        sy[ch, m] = go(SY.at[ch, m], RY.at[ch, m], sy_s.at[ch, m], sy_r.at[ch, m], to)

    def ring_one(ch):
        cs[ch].wait_recv()
        message(ch, 0, y_opp, to_a)
        message(ch, 1, y_b, to_b)

    def ring_two(ch):
        sy[ch, 0].wait_recv()
        message(ch, 2, y_a, to_a, plus=0)

    swaps = lambda ch: rc(PS.at[ch], PR.at[ch], ps_s.at[ch], ps_r.at[ch], x_to[2])

    def activate(ch):
        sy[ch, 1].wait_recv()
        sy[ch, 2].wait_recv()

        def body(i, carry):
            cols = [pl.ds(pl.multiple_of(k * FF + i * 128, 128), 128) for k in range(3)]

            def total(col):
                v = part(ch, y, col)
                return v + RY[ch, 1, :, col].astype(F32) + RY[ch, 2, :, col].astype(F32)

            gate, up, back = [total(col) for col in cols]
            sig = jax.nn.sigmoid(gate)
            silu = gate * sig
            PS[ch, :, cols[0]] = (silu * up).astype(BF)
            PS[ch, :, cols[1]] = (back * up * sig * (1.0 + gate * (1.0 - sig))).astype(BF)
            PS[ch, :, cols[2]] = (back * silu).astype(BF)
            return carry

        lax.fori_loop(0, 6, body, 0)

        @pl.when(c == 1)
        def _():
            swaps(ch).start()
            AH[ch, y] = PS[ch, :, FF:]
            for n, to in ((0, to_a), (1, to_b), (2, peer)):
                ah(ch, n, y, to).start()

        @pl.when(c == 0)
        def _():
            AB[0, ch, y] = PS[ch]
            for n, to in ((0, to_a), (1, to_b), (2, peer)):
                ag(ch, n, y, to).start()

    def ag(ch, n, yy, to):
        block = AB.at[c, ch, yy]
        return rc(block, block, ag_s.at[ch, n], ag_r.at[ch, n], to)

    def ah(ch, n, yy, to):
        block = AH.at[ch, yy]
        return rc(block, block, ah_s.at[ch, n], ah_r.at[ch, n], to)

    def ag_in(ch, n):
        block = AB.at[other if n in (2, 4, 5, 6) else c, ch, y]
        return rc(block, block, ag_s.at[ch, n], ag_r.at[ch, n], peer)

    def choose(ch):
        @pl.when(c == 1)
        def _():
            swaps(ch).wait_recv()

            def body(col):
                keep = jnp.full((48, 256), plan[dp].astype(F32)) > 0.5
                v = jnp.where(keep, PR[ch, :, col].astype(F32), PS[ch, :, col].astype(F32))
                AB[1, ch, y, :, col] = v.astype(BF)

            tiles(body)
            for n, to in ((0, to_a), (1, to_b), (2, peer)):
                ag(ch, n, y, to).start()

    def ag_pass(ch):
        @pl.when(c == 1)
        def _():
            ah(ch, 0, y_b, to_a).wait_recv()
            ah(ch, 3, y_b, to_a).start()
            ah(ch, 4, y_b, peer).start()
            ah(ch, 1, y_a, to_b).wait_recv()
            ah(ch, 5, y_a, peer).start()

        ag_in(ch, 0).wait_recv()
        ag(ch, 3, y_b, to_a).start()
        ag(ch, 4, y_b, peer).start()
        ag_in(ch, 1).wait_recv()
        ag(ch, 5, y_a, peer).start()

    def ag_end(ch):
        @pl.when(c == 1)
        def _():
            ah(ch, 3, y_opp, to_a).wait_recv()
            ah(ch, 6, y_opp, peer).start()

        ag_in(ch, 3).wait_recv()
        ag(ch, 6, y_opp, peer).start()

    def ag_done(ch):
        @pl.when(c == 0)
        def _():
            for n in (2, 4, 5, 6):
                ah(ch, n, y, peer).wait_recv()

        for n in (2, 4, 5, 6):
            ag_in(ch, n).wait_recv()

    rx = {}

    def back_rows(ch):
        for e in (0, 1):
            gd = (AB[0, ch, :, :, FF : 2 * FF] if e == 0 else AH[ch, :, :, :FF]).reshape(192, FF)
            ud = (AB[0, ch, :, :, 2 * FF :] if e == 0 else AH[ch, :, :, FF:]).reshape(192, FF)
            for n in (0, 256):
                res = dot_nt(gd, wg[e, n : n + 256, :]) + dot_nt(ud, wu[e, n : n + 256, :])
                R[ch, e, :, :, n : n + 256] = res.astype(BF).reshape(4, 48, 256)
        for j in (1, 2, 3):
            rx[ch, j] = go(R.at[ch, :, lax.rem(x + j, NX)], RB.at[ch, j], rx_s.at[ch, j - 1], rx_r.at[ch, j - 1], x_to[j])

    rz = {}

    def spread(ch):
        for j in (1, 2, 3):
            rx[ch, j].wait_recv()
        za, zb = lax.rem(z + 8 - ch, NZ), lax.rem(z + 1 + ch, NZ)
        pieces = []
        for s in range(8):
            r0 = RK2[s, pl.ds(za, 1), :]
            r1 = RK2[s, pl.ds(zb, 1), :] + 24.0
            pieces.append(jnp.where(slot_i == jnp.concatenate([r0, r1], axis=1), 1.0, 0.0).astype(BF))
        own = dot_tn(jnp.concatenate(pieces[:2], axis=0), R[ch, :, pl.ds(x, 1)].reshape(96, 512))
        rest = dot_tn(jnp.concatenate(pieces[2:], axis=0), RB[ch, 1:].reshape(288, 512))
        v = own + rest
        for i, d in ((0, (8 - ch) % 8), (1, ch + 1)):
            block = v[128 * i : 128 * i + 128]
            if d == 0:
                OWN[...] = block
            else:
                DS[d] = block.astype(BF)
                rz[d] = go(DS.at[d], ZR.at[d], rz_s.at[d], rz_r.at[d], z_to[d])

    def input_grads(slot, i):
        def inputs(n, carry):
            d = pl.ds(pl.multiple_of(n * 256, 256), 256)
            xs = X[i, :, :, d].reshape(FF, 256)
            for k, out in ((1, gg_o), (2, ug_o)):
                act = AB[slot, :, :, :, k * FF : (k + 1) * FF].reshape(FF, FF)
                out[slot, d, :] = dot_tn(xs, act).astype(BF)
            return carry

        lax.fori_loop(0, 2, inputs, 0)

    def hidden_grads(slot, i):
        def hidden(n, carry):
            f = pl.ds(pl.multiple_of(n * 256, 256), 256)
            hid = AB[slot, :, :, :, f].reshape(FF, 256)
            dg_o[slot, f, :] = dot_tn(hid, G[i].reshape(FF, 512)).astype(BF)
            return carry

        lax.fori_loop(0, 3, hidden, 0)

    def forward(ch):
        pick(ch)
        project(ch)

    hop(1)
    all_places()
    forward(0)
    ring_one(0)
    hop(2)
    ring_two(0)
    forward(1)
    activate(0)
    ring_one(1)
    choose(0)
    hop(3)
    ring_two(1)
    ag_pass(0)
    forward(2)
    activate(1)
    ring_one(2)
    ag_end(0)
    choose(1)
    ring_two(2)
    ag_done(0)
    back_rows(0)
    ag_pass(1)
    hop(4)
    forward(3)
    activate(2)
    ring_one(3)
    ag_end(1)
    choose(2)
    spread(0)
    ring_two(3)
    ag_done(1)
    back_rows(1)
    ag_pass(2)
    activate(3)
    spread(1)
    ag_end(2)
    choose(3)
    ag_done(2)
    back_rows(2)
    ag_pass(3)
    spread(2)
    ag_end(3)
    ag_done(3)
    back_rows(3)
    hidden_grads(1, 2)
    spread(3)
    input_grads(1, 2)
    input_grads(0, 0)
    hidden_grads(0, 0)

    total = OWN[...]
    for d in (1, 7, 2, 6, 3, 5, 4):
        rz[d].wait_recv()
        total = total + ZR[d].astype(F32)
    tg_o[...] = total.astype(BF)
    for copy in sent:
        copy.wait_send()
    for ch in range(4):
        for n in range(7):
            ag(ch, n, y, peer).wait_send()

        @pl.when(c == 1)
        def _():
            swaps(ch).wait_send()
            for n in range(7):
                ah(ch, n, y, peer).wait_send()


def shards(tokens, cotangent, expert_ids, gate_values, swap_plan, gate_weight, up_weight, down_weight):
    vmem = pl.BlockSpec(memory_space=pltpu.VMEM)
    dma = lambda *shape: [pltpu.SemaphoreType.DMA(shape), pltpu.SemaphoreType.DMA(shape)]
    w = 3 * FF
    return pl.pallas_call(
        kernel,
        out_shape=(
            jax.ShapeDtypeStruct(tokens.shape, BF),
            jax.ShapeDtypeStruct(gate_weight.shape, BF),
            jax.ShapeDtypeStruct(up_weight.shape, BF),
            jax.ShapeDtypeStruct(down_weight.shape, BF),
        ),
        in_specs=[pl.BlockSpec(memory_space=pltpu.SMEM)] + [vmem] * 7,
        out_specs=(vmem,) * 4,
        scratch_shapes=[
            pltpu.VMEM((32, 128, 512), BF),
            pltpu.VMEM((32, 128, 512), BF),
            pltpu.VMEM((8, 4, 16, 128), F32),
            pltpu.VMEM((3, 4, 192, 512), BF),
            pltpu.VMEM((3, 4, 192, 512), BF),
            pltpu.VMEM((3, 32, 128), F32),
            pltpu.VMEM((3, 32, 128), F32),
            pltpu.VMEM((8, 8, 128), F32),
            pltpu.VMEM((4, 192, w), BF),
            pltpu.VMEM((4, 192, w), BF),
            pltpu.VMEM((2, 192, w), F32),
            pltpu.VMEM((4, 3, 48, w), BF),
            pltpu.VMEM((4, 3, 48, w), BF),
            pltpu.VMEM((4, 48, w), BF),
            pltpu.VMEM((4, 48, w), BF),
            pltpu.VMEM((2, 4, 4, 48, w), BF),
            pltpu.VMEM((4, 4, 48, 2 * FF), BF),
            pltpu.VMEM((4, 2, 4, 48, 512), BF),
            pltpu.VMEM((4, 4, 2, 48, 512), BF),
            pltpu.VMEM((8, 128, 512), BF),
            pltpu.VMEM((8, 128, 512), BF),
            pltpu.VMEM((128, 512), F32),
        ]
        + dma(3)
        + dma(8)
        + dma(3)
        + dma(2, 4, 4)
        + dma(2, 4)
        + dma(3, 8)
        + dma(4)
        + dma(4, 3)
        + dma(4)
        + dma(4, 7)
        + dma(4, 7)
        + dma(4, 3)
        + dma(8),
        compiler_params=pltpu.CompilerParams(
            collective_id=0, has_side_effects=True, vmem_limit_bytes=62 << 20
        ),
        cost_estimate=pl.CostEstimate(flops=10_000_000_000, bytes_accessed=10_000_000, transcendentals=0),
        name="expert_layer",
    )(
        swap_plan, tokens, cotangent, expert_ids.T, gate_values.T, gate_weight, up_weight, down_weight
    )


def solution(mesh):
    return jax.shard_map(
        shards,
        mesh=mesh,
        in_specs=(
            P("dp", "expert"),
            P("dp", "expert"),
            P("dp", None),
            P("dp", None),
            P(),
            P("dp", "expert", None),
            P("dp", "expert", None),
            P("dp", None, "expert"),
        ),
        out_specs=(
            P("dp", "expert"),
            P("dp", "expert", None),
            P("dp", "expert", None),
            P("dp", None, "expert"),
        ),
        check_vma=False,
    )
```

time: 580 us -> 171 us (0.29)
  waiting for transfers between devices: 329 us -> 0 us
  Pallas kernels: 0 us -> 163 us
  local copies, waits for them, and re-layouts: 97 us -> 7.46 us
  blocking collectives: 51.2 us -> 0 us
  other arithmetic: 36.5 us -> 0 us
  matrix products: 24.8 us -> 0 us
  starting transfers between devices: 22.3 us -> 0 us
  between operations: 15.8 us -> 0.65 us
    pallas_call x0 -> x1, Pallas kernels: none -> 163 us  [shards(): pl.pallas_call(kernel, out_shape=(jax.ShapeDtypeStruct(tokens.shape, BF),...]
    unnamed x3 -> x0, waiting for transfers between devices: 162 us -> none
    all_to_all x2 -> x0, waiting for transfers between devices: 62.6 us -> none  [the longest x1 62.6 us: shards(): lax.all_to_all(rows_acc.reshape(dp_size, most_rows, per_host, width_part)...]
    ppermute x3 -> x0, waiting for transfers between devices: 56.9 us -> none  [from_partner(): return lax.ppermute(block, axis, route)]
    all_to_all x1 -> x0, blocking collectives: 51.2 us -> none  [shards(): lax.all_to_all(token_send, 'dp', split_axis=0, concat_axis=0, tiled=True)]
    all_gather x1 -> x0, waiting for transfers between devices: 46.8 us -> none  [shards(): piece = lax.all_gather(acts, 'expert', axis=0, tiled=True)]
    gather x6 -> x0, local copies, waits for them, and re-layouts: 29.5 us -> none  [the longest x2 9.04 us: shards(): tokens[source // top_count]]
    dot_general x8 -> x0, matrix products: 24.8 us -> none  [the longest x1 4.4 us: shards(): jnp.einsum('rsd,rsf->sdf', x_part, up_part, preferred_element_type=jnp.fl...]
  transfers between devices with their start and end apart: 7 -> 0, of which waited for: 6 -> 0; matrix products, arithmetic and copies ran while one was open for 5% -> 0% of each run, Pallas kernels for 0% -> 0%
where the time goes in v2:
time: 171 us
  Pallas kernels  163 us (95%)
  local copies, waits for them, and re-layouts  7.46 us (4%)
    pallas_call x1, Pallas kernels, shards(): pl.pallas_call(kernel, out_shape=(jax.ShapeDtypeStruct(tokens.shape, BF),...  163 us
    unnamed x8, local copies, waits for them, and re-layouts  7.46 us

profile of v2, /device:TPU:32, one launch (start us, length us, event | category | flops | bytes accessed | tf_op | source)
XLA Modules:
  0.0 170.8 jit_solution(8028074745313568246)
XLA Ops:
  0.6 162.7 %expert_layer.1 = (bf16[128,512]{1,0:T(8,128)(2,1)}, bf16[2,512,768]{2,1,0:T(8,128)(2,1)}, bf16[2,512,768]{2,1,0:T(8,128)(2,1)}, bf16[2,768,512]{2,1,0:T(8,128)(2,1)}) custom-call(s32[32]{0:T(128)} %plan.1, bf16[128,512]{1,0:T(8,128)(2,1)} %tok.1, bf16[128,512]{1,0:T(8,128)(2,1)} %cot.1, s32[8,128]{1,0:T(8,128)} %bitcast.2, f32[8,128]{1,0:T(8,128)} %bitcast.3, ...), custom_call_target="tpu_custom_call" | custom-call | flops 10000000000 | bytes 10000000 | tf_op jit(solution)/shard_map/expert_layer/pallas_call | solution.py:466
  163.4 1.6 copy.16
  164.9 0.0 copy-start.1
  164.9 2.8 %copy.17 = bf16[2,512,768]{2,1,0:T(8,128)(2,1)} copy(bf16[2,512,768]{2,1,0:T(8,128)(2,1)} %get-tuple-element.9) | data formatting | bytes 3145728
  167.7 0.0 copy-done.1
  167.7 0.0 copy-start
  167.7 1.1 copy.18
  168.9 0.8 copy-done
  169.7 1.1 copy.19
Async XLA Ops:
  164.9 2.8 %copy-start.1 = (bf16[2,512,768]{2,1,0:T(8,128)(2,1)S(1)}, bf16[2,512,768]{2,1,0:T(8,128)(2,1)}, u32[]{:S(2)}) copy-start(bf16[2,512,768]{2,1,0:T(8,128)(2,1)} %get-tuple-element.10) | copy-start | bytes 4718596
  167.7 2.0 %copy-start = (bf16[2,768,512]{2,1,0:T(8,128)(2,1)S(1)}, bf16[2,768,512]{2,1,0:T(8,128)(2,1)}, u32[]{:S(2)}) copy-start(bf16[2,768,512]{2,1,0:T(8,128)(2,1)} %get-tuple-element.11) | copy-start | bytes 4718596

commit v3 on v2

--- a/solution.py
+++ b/solution.py
@@ -27,9 +27,10 @@
 
 
 def kernel(
-    plan, tok, cot, ids_in, gates_in, wg, wu, wd,
-    tg_o, gg_o, ug_o, dg_o,
-    T, C, M, X, G, RK, GV, RK2, CS, CR, H, SY, RY, PS, PR, AB, AH, R, RB, DS, ZR, OWN,
+    plan, tok, cot, ids_in, gates_in, wg_in, wu_in, wd_in,
+    tg_out, gg_out, ug_out, dg_out,
+    wg, wu, wd, tg_o, gg_o, ug_o, dg_o, near_s,
+    T, C, M, M2, MF, X, G, RK, GV, RK2, CS, CR, H, SY, RY, PS, PR, AB, AH, R, RB, DS, ZR, OWN,
     mx_s, mx_r, mz_s, mz_r, ax_s, ax_r, az_s, az_r, bz_s, bz_r, bx_s, bx_r, cs_s, cs_r,
     sy_s, sy_r, ps_s, ps_r, ag_s, ag_r, ah_s, ah_r, rx_s, rx_r, rz_s, rz_r,
 ):
@@ -49,6 +50,17 @@
     x_to = [None] + [(at(x + j, z), ex) for j in (1, 2, 3)]
     z_to = [None] + [(at(x, z + i), ex) for i in range(1, NZ)]
 
+    moves = [(wg_in, wg), (wu_in, wu), (wd_in, wd)]
+    moves += [(gg_o.at[0], gg_out.at[0]), (ug_o.at[0], ug_out.at[0]), (dg_o.at[1], dg_out.at[1])]
+    moves += [(gg_o.at[1], gg_out.at[1]), (ug_o.at[1], ug_out.at[1]), (dg_o.at[0], dg_out.at[0])]
+    moves += [(tg_o, tg_out)]
+
+    def local(n):
+        return pltpu.make_async_copy(moves[n][0], moves[n][1], near_s.at[n])
+
+    for n in range(3):
+        local(n).start()
+
     barrier = pltpu.get_barrier_semaphore()
     group = [peer, to_a, to_b] + x_to[1:] + z_to[1:]
     for device in group:
@@ -86,10 +98,14 @@
 
     def send_bx(d):
         b = at(x, z + d)
-        for j in (1, 2, 3):
-            bx[j, d] = go(
-                C.at[b] if d else cot, C.at[b], bx_s.at[j - 1, d], bx_r.at[j - 1, d], x_to[j]
-            )
+        for n, to in ((0, x_to[1]), (1, x_to[3])):
+            bx[n, d] = go(C.at[b] if d else cot, C.at[b], bx_s.at[n, d], bx_r.at[n, d], to)
+
+    def pass_bx(d):
+        for n, (off, xx, to) in enumerate(((0, x + 3, x_to[1]), (64, x + 1, x_to[3]))):
+            bx[n, d].wait_recv()
+            piece = C.at[at(xx, z + d), pl.ds(off, 64)]
+            bx[2 + n, d] = go(piece, piece, bx_s.at[2 + n, d], bx_r.at[2 + n, d], to)
 
     def last(way, j):
         return 4 if (j + way) % 2 == 0 else 3
@@ -106,33 +122,44 @@
     for j in (1, 2, 3):
         mx[j].wait_recv()
     for i in range(1, NZ):
-        mz[i] = go(M.at[z], M.at[z], mz_s.at[i], mz_r.at[i], z_to[i])
+        part_m = M.at[z, pl.ds(2 * c, 2)]
+        mz[i] = go(part_m, part_m, mz_s.at[i], mz_r.at[i], z_to[i])
     send_az(0, 0, 1)
     send_az(1, 0, 1)
     T[dp] = tok[...]
     C[dp] = cot[...]
-    for j in (1, 2, 3):
+
+    def hop_ax(j):
         ax[j].wait_recv()
         send_az(0, j, 1)
         send_az(1, j, 1)
 
-    def hop(h):
+    def hop_b(h):
         for way in (0, 1):
             if h <= 4 - way:
                 bz[way, h].wait_recv()
                 if h < 4 - way:
                     send_bz(way, h + 1)
                 send_bx(8 - h if way == 0 else h)
-        for j in range(4):
+
+    def hop_a(h, *js):
+        for j in js:
             for way in (0, 1):
                 if h <= last(way, j):
                     az[way, j, h].wait_recv()
                     if h < last(way, j):
                         send_az(way, j, h + 1)
 
-    def all_places():
+    def places_out():
         for i in range(1, NZ):
             mz[i].wait_recv()
+        part_m = M.at[:, pl.ds(2 * c, 2)]
+        mz[0] = go(part_m, M2, mz_s.at[0], mz_r.at[0], peer)
+
+    def all_places():
+        mz[0].wait_recv()
+        MF[:, pl.ds(2 * c, 2)] = M[:, pl.ds(2 * c, 2)]
+        MF[:, pl.ds(2 * other, 2)] = M2[...]
         flag = jnp.full((1, 128), plan[dp].astype(F32))
         far = lax.rem(dp + NX * NZ // 2, NX * NZ)
         own_id = (2 * dp + 1).astype(F32)
@@ -146,13 +173,13 @@
             hit = jnp.sum(jnp.where(match, 1.0, 0.0), axis=1)
             return match, jnp.where(hit > 0.0, dot(hit.astype(BF), upper) - 1.0, -1000.0)
 
-        ids = M[:, :, 0:8, :].reshape(32, 8, 128)
-        gates = M[:, :, 8:16, :].reshape(32, 8, 128)
+        ids = MF[:, :, 0:8, :].reshape(32, 8, 128)
+        gates = MF[:, :, 8:16, :].reshape(32, 8, 128)
         for i, target in enumerate(((2 * dp).astype(F32), own_id, star_id[:, None, :])):
             match, rank = places(ids, target)
             RK[i] = rank
             GV[i] = jnp.sum(jnp.where(match, gates, 0.0), axis=1)
-        near = M[:, pl.ds(x, 1), 0:8, :].reshape(8, 8, 128)
+        near = MF[:, pl.ds(x, 1), 0:8, :].reshape(8, 8, 128)
         for j in range(4):
             for e in (0, 1):
                 _, rank = places(near, (2 * at(x + 4 - j, z) + e).astype(F32))
@@ -169,8 +196,8 @@
 
     def pick(ch):
         for d in {(8 - ch) % 8, ch + 1}:
-            for j in (1, 2, 3):
-                bx[j, d].wait_recv()
+            for n in (2, 3):
+                bx[n, d].wait_recv()
 
         def step(j, carry):
             ba, bb = at(j, z + 8 - ch), at(j, z + 1 + ch)
@@ -282,10 +309,6 @@
         block = AH.at[ch, yy]
         return rc(block, block, ah_s.at[ch, n], ah_r.at[ch, n], to)
 
-    def ag_in(ch, n):
-        block = AB.at[other if n in (2, 4, 5, 6) else c, ch, y]
-        return rc(block, block, ag_s.at[ch, n], ag_r.at[ch, n], peer)
-
     def choose(ch):
         @pl.when(c == 1)
         def _():
@@ -300,38 +323,43 @@
             for n, to in ((0, to_a), (1, to_b), (2, peer)):
                 ag(ch, n, y, to).start()
 
-    def ag_pass(ch):
-        @pl.when(c == 1)
-        def _():
-            ah(ch, 0, y_b, to_a).wait_recv()
-            ah(ch, 3, y_b, to_a).start()
-            ah(ch, 4, y_b, peer).start()
-            ah(ch, 1, y_a, to_b).wait_recv()
-            ah(ch, 5, y_a, peer).start()
-
-        ag_in(ch, 0).wait_recv()
-        ag(ch, 3, y_b, to_a).start()
-        ag(ch, 4, y_b, peer).start()
-        ag_in(ch, 1).wait_recv()
-        ag(ch, 5, y_a, peer).start()
-
-    def ag_end(ch):
-        @pl.when(c == 1)
-        def _():
-            ah(ch, 3, y_opp, to_a).wait_recv()
-            ah(ch, 6, y_opp, peer).start()
-
-        ag_in(ch, 3).wait_recv()
-        ag(ch, 6, y_opp, peer).start()
-
-    def ag_done(ch):
-        @pl.when(c == 0)
-        def _():
-            for n in (2, 4, 5, 6):
-                ah(ch, n, y, peer).wait_recv()
-
+    def pass_on(block, ch):
+        block(ch, 0, y_b, to_a).wait_recv()
+        block(ch, 3, y_b, to_a).start()
+        block(ch, 4, y_b, peer).start()
+        block(ch, 1, y_a, to_b).wait_recv()
+        block(ch, 5, y_a, peer).start()
+
+    def pass_end(block, ch):
+        block(ch, 3, y_opp, to_a).wait_recv()
+        block(ch, 6, y_opp, peer).start()
+
+    def on_cores(zero, one):
+        if zero is not None:
+            pl.when(c == 0)(zero)
+        pl.when(c == 1)(one)
+
+    def tok_pass(ch):
+        on_cores(lambda: pass_on(ag, ch), lambda: pass_on(ah, ch))
+
+    def tok_end(ch):
+        on_cores(lambda: pass_end(ag, ch), lambda: pass_end(ah, ch))
+
+    def peer_in(block, ch):
         for n in (2, 4, 5, 6):
-            ag_in(ch, n).wait_recv()
+            block(ch, n, y, peer).wait_recv()
+
+    def tok_done(ch):
+        on_cores(lambda: peer_in(ah, ch), lambda: peer_in(ag, ch))
+
+    def star_pass(ch):
+        on_cores(None, lambda: pass_on(ag, ch))
+
+    def star_end(ch):
+        on_cores(None, lambda: pass_end(ag, ch))
+
+    def star_done(ch):
+        pl.when(c == 0)(lambda: peer_in(ag, ch))
 
     rx = {}
 
@@ -391,61 +419,102 @@
         pick(ch)
         project(ch)
 
-    hop(1)
+    hop_ax(1)
+    hop_ax(3)
+    hop_b(1)
+    hop_ax(2)
+    pass_bx(0)
+    hop_a(1, 0)
+    hop_b(2)
+    hop_a(1, 1)
+    places_out()
+    pass_bx(7)
+    pass_bx(1)
+    hop_a(1, 3)
+    hop_b(3)
+    for n in range(3):
+        local(n).wait()
     all_places()
+    hop_a(1, 2)
     forward(0)
+    pass_bx(6)
+    pass_bx(2)
+    hop_a(2, 0, 1)
+    hop_b(4)
     ring_one(0)
-    hop(2)
+    hop_a(2, 3, 2)
+    pass_bx(5)
+    pass_bx(3)
     ring_two(0)
     forward(1)
+    pass_bx(4)
     activate(0)
     ring_one(1)
-    choose(0)
-    hop(3)
+    tok_pass(0)
     ring_two(1)
-    ag_pass(0)
+    hop_a(3, 0, 1, 3, 2)
     forward(2)
+    tok_end(0)
     activate(1)
     ring_one(2)
-    ag_end(0)
-    choose(1)
+    choose(0)
+    tok_done(0)
+    back_rows(0)
+    tok_pass(1)
     ring_two(2)
-    ag_done(0)
-    back_rows(0)
-    ag_pass(1)
-    hop(4)
+    hop_a(4, 0, 1, 3, 2)
     forward(3)
+    tok_end(1)
     activate(2)
     ring_one(3)
-    ag_end(1)
+    star_pass(0)
+    choose(1)
+    tok_done(1)
+    back_rows(1)
+    spread(0)
+    tok_pass(2)
+    ring_two(3)
+    star_end(0)
+    star_pass(1)
     choose(2)
-    spread(0)
-    ring_two(3)
-    ag_done(1)
-    back_rows(1)
-    ag_pass(2)
+    tok_end(2)
     activate(3)
+    tok_done(2)
+    back_rows(2)
     spread(1)
-    ag_end(2)
+    tok_pass(3)
+    star_end(1)
+    star_pass(2)
     choose(3)
-    ag_done(2)
-    back_rows(2)
-    ag_pass(3)
     spread(2)
-    ag_end(3)
-    ag_done(3)
+    tok_end(3)
+    star_end(2)
+    tok_done(3)
     back_rows(3)
+    star_pass(3)
+    hidden_grads(0, 0)
+    local(8).start()
+    spread(3)
+    star_end(3)
+    input_grads(0, 0)
+    local(3).start()
+    local(4).start()
+    for ch in range(4):
+        star_done(ch)
     hidden_grads(1, 2)
-    spread(3)
+    local(5).start()
     input_grads(1, 2)
-    input_grads(0, 0)
-    hidden_grads(0, 0)
+    local(6).start()
+    local(7).start()
 
     total = OWN[...]
     for d in (1, 7, 2, 6, 3, 5, 4):
         rz[d].wait_recv()
         total = total + ZR[d].astype(F32)
     tg_o[...] = total.astype(BF)
+    local(9).start()
+    for n in range(3, 10):
+        local(n).wait()
     for copy in sent:
         copy.wait_send()
     for ch in range(4):
@@ -459,11 +528,27 @@
                 ah(ch, n, y, peer).wait_send()
 
 
+def hand_out(tg, gg, ug, dg, tg_o, gg_o, ug_o, dg_o, tg_v, gg_v, ug_v, dg_v, sem):
+    steps = [(tg, tg_v, tg_o)]
+    for src, mid, dst in ((gg, gg_v, gg_o), (ug, ug_v, ug_o), (dg, dg_v, dg_o)):
+        steps += [(src.at[e], mid.at[e], dst.at[e]) for e in (0, 1)]
+    first = [pltpu.make_async_copy(a, b, sem.at[0, n]) for n, (a, b, _) in enumerate(steps)]
+    then = [pltpu.make_async_copy(b, d, sem.at[1, n]) for n, (_, b, d) in enumerate(steps)]
+    for copy in first:
+        copy.start()
+    for one, two in zip(first, then):
+        one.wait()
+        two.start()
+    for copy in then:
+        copy.wait()
+
+
 def shards(tokens, cotangent, expert_ids, gate_values, swap_plan, gate_weight, up_weight, down_weight):
     vmem = pl.BlockSpec(memory_space=pltpu.VMEM)
+    hbm = pl.BlockSpec(memory_space=pl.ANY)
     dma = lambda *shape: [pltpu.SemaphoreType.DMA(shape), pltpu.SemaphoreType.DMA(shape)]
     w = 3 * FF
-    return pl.pallas_call(
+    outs = pl.pallas_call(
         kernel,
         out_shape=(
             jax.ShapeDtypeStruct(tokens.shape, BF),
@@ -471,11 +556,21 @@
             jax.ShapeDtypeStruct(up_weight.shape, BF),
             jax.ShapeDtypeStruct(down_weight.shape, BF),
         ),
-        in_specs=[pl.BlockSpec(memory_space=pltpu.SMEM)] + [vmem] * 7,
-        out_specs=(vmem,) * 4,
+        in_specs=[pl.BlockSpec(memory_space=pltpu.SMEM)] + [vmem] * 4 + [hbm] * 3,
+        out_specs=(hbm,) * 4,
         scratch_shapes=[
+            pltpu.VMEM(gate_weight.shape, BF),
+            pltpu.VMEM(up_weight.shape, BF),
+            pltpu.VMEM(down_weight.shape, BF),
+            pltpu.VMEM(tokens.shape, BF),
+            pltpu.VMEM(gate_weight.shape, BF),
+            pltpu.VMEM(up_weight.shape, BF),
+            pltpu.VMEM(down_weight.shape, BF),
+            pltpu.SemaphoreType.DMA((10,)),
             pltpu.VMEM((32, 128, 512), BF),
             pltpu.VMEM((32, 128, 512), BF),
+            pltpu.VMEM((8, 4, 16, 128), F32),
+            pltpu.VMEM((8, 2, 16, 128), F32),
             pltpu.VMEM((8, 4, 16, 128), F32),
             pltpu.VMEM((3, 4, 192, 512), BF),
             pltpu.VMEM((3, 4, 192, 512), BF),
@@ -502,7 +597,7 @@
         + dma(3)
         + dma(2, 4, 4)
         + dma(2, 4)
-        + dma(3, 8)
+        + dma(4, 8)
         + dma(4)
         + dma(4, 3)
         + dma(4)
@@ -518,6 +613,14 @@
     )(
         swap_plan, tokens, cotangent, expert_ids.T, gate_values.T, gate_weight, up_weight, down_weight
     )
+    return pl.pallas_call(
+        hand_out,
+        out_shape=tuple(jax.ShapeDtypeStruct(o.shape, o.dtype) for o in outs),
+        in_specs=[hbm] * 4,
+        out_specs=(hbm,) * 4,
+        scratch_shapes=[pltpu.VMEM(o.shape, o.dtype) for o in outs] + [pltpu.SemaphoreType.DMA((2, 7))],
+        name="hand_out",
+    )(*outs)
 
 
 def solution(mesh):

time: 171 us -> 156 us (0.912)
  Pallas kernels: 163 us -> 155 us
  local copies, waits for them, and re-layouts: 7.46 us -> 0 us
    pallas_call x1, Pallas kernels: 163 us -> 151 us  [shards(): pl.pallas_call(kernel, out_shape=(jax.ShapeDtypeStruct(tokens.shape, BF),...]
    unnamed x8 -> x0, local copies, waits for them, and re-layouts: 7.46 us -> none
    pallas_call x0 -> x1, Pallas kernels: none -> 4.2 us  [shards(): pl.pallas_call(hand_out, out_shape=tuple((jax.ShapeDtypeStruct(o.shape, o...]
where the time goes in v3:
time: 156 us
  Pallas kernels  155 us (99%)
    pallas_call x1, Pallas kernels, shards(): pl.pallas_call(kernel, out_shape=(jax.ShapeDtypeStruct(tokens.shape, BF),...  151 us
    pallas_call x1, Pallas kernels, shards(): pl.pallas_call(hand_out, out_shape=tuple((jax.ShapeDtypeStruct(o.shape, o...  4.2 us

profile of v3, /device:TPU:32, one launch (start us, length us, event | category | flops | bytes accessed | tf_op | source)
XLA Modules:
  0.0 156.0 jit_solution(9412227863693646844)
XLA Ops:
  0.6 151.0 %expert_layer.1 = (bf16[128,512]{1,0:T(8,128)(2,1)}, bf16[2,512,768]{2,1,0:T(8,128)(2,1)}, bf16[2,512,768]{2,1,0:T(8,128)(2,1)}, bf16[2,768,512]{2,1,0:T(8,128)(2,1)}) custom-call(s32[32]{0:T(128)} %plan.1, bf16[128,512]{1,0:T(8,128)(2,1)} %tok.1, bf16[128,512]{1,0:T(8,128)(2,1)} %cot.1, s32[8,128]{1,0:T(8,128)} %bitcast.2, f32[8,128]{1,0:T(8,128)} %bitcast.3, ...), custom_call_target="tpu_custom_call" | custom-call | flops 10000000000 | bytes 10000000 | tf_op jit(solution)/shard_map/expert_layer/pallas_call | solution.py:551
  151.6 4.2 %hand_out.1 = (bf16[128,512]{1,0:T(8,128)(2,1)}, bf16[2,512,768]{2,1,0:T(8,128)(2,1)}, bf16[2,512,768]{2,1,0:T(8,128)(2,1)}, bf16[2,768,512]{2,1,0:T(8,128)(2,1)}) custom-call(bf16[128,512]{1,0:T(8,128)(2,1)} %get-tuple-element.8.tg, bf16[2,512,768]{2,1,0:T(8,128)(2,1)} %get-tuple-element.9.gg, bf16[2,512,768]{2,1,0:T(8,128)(2,1)} %get-tuple-element.10.ug, ...), custom_call_target="tpu_custom_call" | custom-call | tf_op jit(solution)/shard_map/hand_out/pallas_call | solution.py:616

commit v4 on v3

--- a/solution.py
+++ b/solution.py
@@ -12,6 +12,7 @@
 MESH = pl.DeviceIdType.MESH
 NX, NZ, NY = 4, 8, 4
 FF = 768
+PAIRS = ((7, 1), (6, 2), (5, 3), (0, 4))
 
 
 def dot(a, b):
@@ -195,14 +196,15 @@
         lax.fori_loop(0, n, step, 0)
 
     def pick(ch):
-        for d in {(8 - ch) % 8, ch + 1}:
+        da, db = PAIRS[ch]
+        for d in (da, db):
             for n in (2, 3):
                 bx[n, d].wait_recv()
 
         def step(j, carry):
-            ba, bb = at(j, z + 8 - ch), at(j, z + 1 + ch)
-            ra = lax.rem(z + 8 - ch, NZ) * 4 + j
-            rb = lax.rem(z + 1 + ch, NZ) * 4 + j
+            ba, bb = at(j, z + da), at(j, z + db)
+            ra = lax.rem(z + da, NZ) * 4 + j
+            rb = lax.rem(z + db, NZ) * 4 + j
             ones, scale = [], []
             for i in range(3):
                 r0 = RK[i, pl.ds(ra, 1), :]
@@ -378,7 +380,8 @@
     def spread(ch):
         for j in (1, 2, 3):
             rx[ch, j].wait_recv()
-        za, zb = lax.rem(z + 8 - ch, NZ), lax.rem(z + 1 + ch, NZ)
+        da, db = PAIRS[ch]
+        za, zb = lax.rem(z + da, NZ), lax.rem(z + db, NZ)
         pieces = []
         for s in range(8):
             r0 = RK2[s, pl.ds(za, 1), :]
@@ -387,7 +390,7 @@
         own = dot_tn(jnp.concatenate(pieces[:2], axis=0), R[ch, :, pl.ds(x, 1)].reshape(96, 512))
         rest = dot_tn(jnp.concatenate(pieces[2:], axis=0), RB[ch, 1:].reshape(288, 512))
         v = own + rest
-        for i, d in ((0, (8 - ch) % 8), (1, ch + 1)):
+        for i, d in ((1, db), (0, da)):
             block = v[128 * i : 128 * i + 128]
             if d == 0:
                 OWN[...] = block
@@ -474,23 +477,23 @@
     spread(0)
     tok_pass(2)
     ring_two(3)
+    tok_end(2)
     star_end(0)
+    activate(3)
     star_pass(1)
     choose(2)
-    tok_end(2)
-    activate(3)
     tok_done(2)
     back_rows(2)
     spread(1)
     tok_pass(3)
     star_end(1)
+    choose(3)
+    tok_end(3)
     star_pass(2)
-    choose(3)
     spread(2)
-    tok_end(3)
-    star_end(2)
     tok_done(3)
     back_rows(3)
+    star_end(2)
     star_pass(3)
     hidden_grads(0, 0)
     local(8).start()

time: 156 us -> 149 us (0.955); the launches traced: 156 us -> 147 us
  Pallas kernels: 155 us -> 146 us
    pallas_call x1, Pallas kernels: 151 us -> 142 us  [shards(): pl.pallas_call(kernel, out_shape=(jax.ShapeDtypeStruct(tokens.shape, BF),...]
where the time goes in v4:
time: 149 us; the launch traced here: 147 us
  Pallas kernels  146 us (98%)
    pallas_call x1, Pallas kernels, shards(): pl.pallas_call(kernel, out_shape=(jax.ShapeDtypeStruct(tokens.shape, BF),...  142 us
    pallas_call x1, Pallas kernels, shards(): pl.pallas_call(hand_out, out_shape=tuple((jax.ShapeDtypeStruct(o.shape, o...  4.2 us

profile of v4, /device:TPU:32, one launch (start us, length us, event | category | flops | bytes accessed | tf_op | source)
XLA Modules:
  0.0 147.3 jit_solution(3870599268198823809)
XLA Ops:
  0.6 142.3 %expert_layer.1 = (bf16[128,512]{1,0:T(8,128)(2,1)}, bf16[2,512,768]{2,1,0:T(8,128)(2,1)}, bf16[2,512,768]{2,1,0:T(8,128)(2,1)}, bf16[2,768,512]{2,1,0:T(8,128)(2,1)}) custom-call(s32[32]{0:T(128)} %plan.1, bf16[128,512]{1,0:T(8,128)(2,1)} %tok.1, bf16[128,512]{1,0:T(8,128)(2,1)} %cot.1, s32[8,128]{1,0:T(8,128)} %bitcast.2, f32[8,128]{1,0:T(8,128)} %bitcast.3, ...), custom_call_target="tpu_custom_call" | custom-call | flops 10000000000 | bytes 10000000 | tf_op jit(solution)/shard_map/expert_layer/pallas_call | solution.py:554
  142.9 4.2 %hand_out.1 = (bf16[128,512]{1,0:T(8,128)(2,1)}, bf16[2,512,768]{2,1,0:T(8,128)(2,1)}, bf16[2,512,768]{2,1,0:T(8,128)(2,1)}, bf16[2,768,512]{2,1,0:T(8,128)(2,1)}) custom-call(bf16[128,512]{1,0:T(8,128)(2,1)} %get-tuple-element.8.tg, bf16[2,512,768]{2,1,0:T(8,128)(2,1)} %get-tuple-element.9.gg, bf16[2,512,768]{2,1,0:T(8,128)(2,1)} %get-tuple-element.10.ug, ...), custom_call_target="tpu_custom_call" | custom-call | tf_op jit(solution)/shard_map/hand_out/pallas_call | solution.py:619

commit v5 on v4

--- a/solution.py
+++ b/solution.py
@@ -365,21 +365,33 @@
 
     rx = {}
 
+    def rows_of(ch, e):
+        gd = (AB[0, ch, :, :, FF : 2 * FF] if e == 0 else AH[ch, :, :, :FF]).reshape(192, FF)
+        ud = (AB[0, ch, :, :, 2 * FF :] if e == 0 else AH[ch, :, :, FF:]).reshape(192, FF)
+        for n in (0, 256):
+            res = dot_nt(gd, wg[e, n : n + 256, :]) + dot_nt(ud, wu[e, n : n + 256, :])
+            R[ch, e, :, :, n : n + 256] = res.astype(BF).reshape(4, 48, 256)
+
+    def send_rows(ch, k, e):
+        for j in (1, 2, 3):
+            rx[ch, k, j] = go(
+                R.at[ch, e, lax.rem(x + j, NX)], RB.at[ch, j, e], rx_s.at[ch, k, j - 1],
+                rx_r.at[ch, k, j - 1], x_to[j],
+            )
+
     def back_rows(ch):
-        for e in (0, 1):
-            gd = (AB[0, ch, :, :, FF : 2 * FF] if e == 0 else AH[ch, :, :, :FF]).reshape(192, FF)
-            ud = (AB[0, ch, :, :, 2 * FF :] if e == 0 else AH[ch, :, :, FF:]).reshape(192, FF)
-            for n in (0, 256):
-                res = dot_nt(gd, wg[e, n : n + 256, :]) + dot_nt(ud, wu[e, n : n + 256, :])
-                R[ch, e, :, :, n : n + 256] = res.astype(BF).reshape(4, 48, 256)
-        for j in (1, 2, 3):
-            rx[ch, j] = go(R.at[ch, :, lax.rem(x + j, NX)], RB.at[ch, j], rx_s.at[ch, j - 1], rx_r.at[ch, j - 1], x_to[j])
+        on_cores(lambda: rows_of(ch, 0), lambda: rows_of(ch, 1))
+        send_rows(ch, 0, c)
+        tok_done(ch)
+        on_cores(lambda: rows_of(ch, 1), lambda: rows_of(ch, 0))
+        send_rows(ch, 1, other)
 
     rz = {}
 
     def spread(ch):
         for j in (1, 2, 3):
-            rx[ch, j].wait_recv()
+            rx[ch, 0, j].wait_recv()
+            rx[ch, 1, j].wait_recv()
         da, db = PAIRS[ch]
         za, zb = lax.rem(z + da, NZ), lax.rem(z + db, NZ)
         pieces = []
@@ -461,7 +473,6 @@
     activate(1)
     ring_one(2)
     choose(0)
-    tok_done(0)
     back_rows(0)
     tok_pass(1)
     ring_two(2)
@@ -472,7 +483,6 @@
     ring_one(3)
     star_pass(0)
     choose(1)
-    tok_done(1)
     back_rows(1)
     spread(0)
     tok_pass(2)
@@ -482,7 +492,6 @@
     activate(3)
     star_pass(1)
     choose(2)
-    tok_done(2)
     back_rows(2)
     spread(1)
     tok_pass(3)
@@ -491,7 +500,6 @@
     tok_end(3)
     star_pass(2)
     spread(2)
-    tok_done(3)
     back_rows(3)
     star_end(2)
     star_pass(3)
@@ -606,7 +614,7 @@
         + dma(4)
         + dma(4, 7)
         + dma(4, 7)
-        + dma(4, 3)
+        + dma(4, 2, 3)
         + dma(8),
         compiler_params=pltpu.CompilerParams(
             collective_id=0, has_side_effects=True, vmem_limit_bytes=62 << 20

time: 149 us -> 149 us (level)
  the two profiles are of different devices: /device:TPU:32 before, /device:TPU:1 now
where the time goes in v5:
time: 149 us
  Pallas kernels  148 us (99%)
    pallas_call x1, Pallas kernels, shards(): pl.pallas_call(kernel, out_shape=(jax.ShapeDtypeStruct(tokens.shape, BF),...  144 us
    pallas_call x1, Pallas kernels, shards(): pl.pallas_call(hand_out, out_shape=tuple((jax.ShapeDtypeStruct(o.shape, o...  4.2 us

profile of v5, /device:TPU:1, one launch (start us, length us, event | category | flops | bytes accessed | tf_op | source)
XLA Modules:
  0.0 149.0 jit_solution(3588823869561592138)
XLA Ops:
  0.6 144.0 %expert_layer.1 = (bf16[128,512]{1,0:T(8,128)(2,1)}, bf16[2,512,768]{2,1,0:T(8,128)(2,1)}, bf16[2,512,768]{2,1,0:T(8,128)(2,1)}, bf16[2,768,512]{2,1,0:T(8,128)(2,1)}) custom-call(s32[32]{0:T(128)} %plan.1, bf16[128,512]{1,0:T(8,128)(2,1)} %tok.1, bf16[128,512]{1,0:T(8,128)(2,1)} %cot.1, s32[8,128]{1,0:T(8,128)} %bitcast.2, f32[8,128]{1,0:T(8,128)} %bitcast.3, ...), custom_call_target="tpu_custom_call" | custom-call | flops 10000000000 | bytes 10000000 | tf_op jit(solution)/shard_map/expert_layer/pallas_call | solution.py:562
  144.6 4.2 %hand_out.1 = (bf16[128,512]{1,0:T(8,128)(2,1)}, bf16[2,512,768]{2,1,0:T(8,128)(2,1)}, bf16[2,512,768]{2,1,0:T(8,128)(2,1)}, bf16[2,768,512]{2,1,0:T(8,128)(2,1)}) custom-call(bf16[128,512]{1,0:T(8,128)(2,1)} %get-tuple-element.8.tg, bf16[2,512,768]{2,1,0:T(8,128)(2,1)} %get-tuple-element.9.gg, bf16[2,512,768]{2,1,0:T(8,128)(2,1)} %get-tuple-element.10.ug, ...), custom_call_target="tpu_custom_call" | custom-call | tf_op jit(solution)/shard_map/hand_out/pallas_call | solution.py:627
